TPU v7x, 256 devices: a whole 4x4x8 slice. The times are simulated.
256 devices in a mesh: box: 32 (over x, y, core), sub: 8 (over z).
Axes of the slice: x: 4, y: 4, z: 8, core: 2. Of those that a mesh axis runs over, the one named last changes fastest.
Arguments:
- source: float32 [256, 32, 4096], P('sub', None, 'box'), may hold values from -8 to 8
- beta: float32 [256, 32, 4096], P('sub', None, 'box'), may hold values from 0.1 to 10
- counts: int32 [32], replicated, may hold values from 1 to 4, 64 in all
Outputs:
- potential: float32 [256, 32, 4096], P('sub', None, 'box')
Inputs may be any that keep to these rules, and one draw needn't show every extreme that they name: Columns are owned in order along x: index i of box owns the counts[i] columns after those of lower indices, in its first slots; the counts sum to 64, and some index owns exactly 4.
All inputs are finite; a program needn't handle non-finite values.
Results may differ from a plain program's by a relative error of at most 0.0001.
Values sent between devices are 32-bit elements; how exact they have to be, the bound alone decides.
A program may use at most 192 MiB of HBM per device.

v0:
```python
import jax
import jax.numpy as jnp
from jax import lax
from jax.sharding import PartitionSpec as P

COL_DEV = 2
CAP = 4
LEVELS = 3
COARSE_SWEEPS = 8


OMEGA = 0.8


def padded_2(block, sides, width, periodic):
    for axis, dim in sides:
        count = lax.axis_size(axis)
        forward = [(i, i + 1) for i in range(count - 1)]
        if periodic:
            forward.append((count - 1, 0))
        backward = [(target, source) for source, target in forward]
        low = lax.ppermute(
            lax.slice_in_dim(block, block.shape[dim] - width, None, axis=dim), axis, forward
        )
        high = lax.ppermute(lax.slice_in_dim(block, 0, width, axis=dim), axis, backward)
        block = jnp.concatenate([low, block, high], axis=dim)
    return block


def shifted_z(field, upward):
    zero_plane = jnp.zeros_like(field[:1])
    if upward:
        return jnp.concatenate([field[1:], zero_plane], 0)
    return jnp.concatenate([zero_plane, field[:-1]], 0)


def global_near(field):
    return (
        jnp.roll(field, 1, 2),
        jnp.roll(field, -1, 2),
        jnp.roll(field, 1, 1),
        jnp.roll(field, -1, 1),
        shifted_z(field, False),
        shifted_z(field, True),
    )


def local_total(values):
    return jnp.sum(values)


def face_coefs(beta_level, nearby):
    beside_all = nearby(beta_level)
    couple = tuple((0.5 * (beta_level + other) for other in beside_all))
    diagonal = couple[0] + couple[1] + couple[2] + couple[3] + couple[4] + couple[5]
    return (couple, diagonal)


def apply_operator(field, nearby, couple, diagonal):
    beside_all = nearby(field)
    total = couple[0] * beside_all[0]
    for which in range(1, 6):
        total = total + couple[which] * beside_all[which]
    return diagonal * field - total


def relax(potential, source_level, nearby, couple, diagonal):
    return (
        potential
        + OMEGA * (source_level - apply_operator(potential, nearby, couple, diagonal)) / diagonal
    )


def children_sum(field):
    plane_count, row_count, col_count = field.shape
    return field.reshape(plane_count // 2, 2, row_count // 2, 2, col_count // 2, 2).sum(
        axis=(1, 3, 5)
    )


def prolong(field):
    return jnp.repeat(jnp.repeat(jnp.repeat(field, 2, 0), 2, 1), 2, 2)


def column_index(counts, columns_total, width):
    ends = jnp.cumsum(counts)
    starts = ends - counts
    column = jnp.arange(columns_total, dtype=jnp.int32)
    owner = jnp.sum((column[:, None] >= ends[None, :]).astype(jnp.int32), axis=1)
    device_ids = jnp.arange(counts.shape[0], dtype=jnp.int32)
    owner_start = jnp.sum(
        jnp.where(owner[:, None] == device_ids[None, :], starts[None, :], 0), axis=1
    )
    base = owner * CAP + column - owner_start
    return (base[:, None] * width + jnp.arange(width, dtype=jnp.int32)[None, :]).reshape(-1)


def make_near(live_width, x_position):

    def local_near(field):
        first_col = field[:, :, 0:1]
        last_col = lax.dynamic_slice_in_dim(field, live_width - 1, 1, 2)
        rim_pair = padded_2(jnp.concatenate([first_col, last_col], 2), (("box", 2),), 1, True)
        left_ghost = rim_pair[:, :, 0:1]
        right_ghost = rim_pair[:, :, 3:4]
        below_x = jnp.concatenate([left_ghost, field[:, :, :-1]], 2)
        above_x = jnp.concatenate([field[:, :, 1:], jnp.zeros_like(first_col)], 2)
        above_x = jnp.where(x_position == live_width - 1, right_ghost, above_x)
        z_padded = padded_2(field, (("sub", 0),), 1, False)
        return (
            below_x,
            above_x,
            jnp.roll(field, 1, 1),
            jnp.roll(field, -1, 1),
            z_padded[:-2],
            z_padded[2:],
        )

    return local_near


def coarse_solve(source_level, beta_level, nearby, total_of):
    couple, diagonal = face_coefs(beta_level, nearby)
    residual = source_level
    direction = residual / diagonal
    norm_now = total_of(residual * residual / diagonal)

    def iterate(repeat, carry):
        potential, residual, direction, norm_now = carry
        image = apply_operator(direction, nearby, couple, diagonal)
        alpha = norm_now / total_of(direction * image)
        potential = potential + alpha * direction
        residual = residual - alpha * image
        scaled = residual / diagonal
        norm_next = total_of(residual * scaled)
        direction = scaled + norm_next / norm_now * direction
        return (potential, residual, direction, norm_next)

    start = (jnp.zeros_like(source_level), residual, direction, norm_now)
    return lax.fori_loop(0, COARSE_SWEEPS, iterate, start)[0]


def coarse_level(source_level, beta_level, counts, my_count, my_start):
    plane_count, row_count, slot_width = source_level.shape
    edge = slot_width // CAP
    box_count = lax.axis_size("box")
    columns = column_index(counts, box_count * COL_DEV, edge)
    stacked = jnp.stack([source_level, beta_level])
    sub_count = lax.axis_size("sub")
    gathered = lax.all_gather(stacked[None], ("box", "sub"), axis=0, tiled=True)
    gathered = gathered.reshape(box_count, sub_count, 2, plane_count, row_count, slot_width)
    gathered = gathered.transpose(2, 1, 3, 4, 0, 5).reshape(
        2, sub_count * plane_count, row_count, box_count * slot_width
    )
    compact = jnp.take(gathered, columns, axis=3)
    solved = coarse_solve(compact[0], compact[1], global_near, local_total)
    mine = lax.dynamic_slice_in_dim(solved, lax.axis_index("sub") * plane_count, plane_count, 0)
    padded = jnp.concatenate([mine, jnp.zeros_like(source_level)], 2)
    part = lax.dynamic_slice_in_dim(padded, my_start * edge, slot_width, 2)
    x_position = lax.broadcasted_iota(jnp.int32, source_level.shape, 2)
    return jnp.where(x_position < my_count * edge, part, 0.0)


def vcycle(level, source_level, beta_level, counts, my_count, my_start):
    if level == LEVELS:
        return coarse_level(source_level, beta_level, counts, my_count, my_start)
    plane_count, row_count, slot_width = source_level.shape
    edge = slot_width // CAP
    live_width = my_count * edge
    x_position = lax.broadcasted_iota(jnp.int32, source_level.shape, 2)
    inside = x_position < live_width
    nearby = make_near(live_width, x_position)
    couple, diagonal = face_coefs(beta_level, nearby)
    diagonal = jnp.where(inside, diagonal, 1.0)

    def smooth(potential):
        potential = jnp.where(inside, relax(potential, source_level, nearby, couple, diagonal), 0.0)
        return potential

    potential = smooth(jnp.zeros_like(source_level))
    residual = jnp.where(
        inside, source_level - apply_operator(potential, nearby, couple, diagonal), 0.0
    )
    correction = vcycle(
        level + 1,
        0.5 * children_sum(residual),
        0.125 * children_sum(beta_level),
        counts,
        my_count,
        my_start,
    )
    potential = potential + prolong(correction)
    return smooth(potential)


def per_device(source, beta, counts):
    device_index = lax.axis_index("box")
    onehot_me = lax.broadcasted_iota(jnp.int32, counts.shape, 0) == device_index
    ends = jnp.cumsum(counts)
    my_count = jnp.sum(jnp.where(onehot_me, counts, 0))
    my_start = jnp.sum(jnp.where(onehot_me, ends - counts, 0))
    edge = source.shape[2] // CAP
    x_position = lax.broadcasted_iota(jnp.int32, source.shape, 2)
    inside = x_position < my_count * edge
    source_live = jnp.where(inside, source, 0.0)
    beta_live = jnp.where(inside, beta, 0.0)
    return vcycle(0, source_live, beta_live, counts, my_count, my_start)


def solution(mesh):
    in_specs = (P("sub", None, "box"), P("sub", None, "box"), P())
    out_specs = P("sub", None, "box")
    return jax.shard_map(
        per_device, mesh=mesh, in_specs=in_specs, out_specs=out_specs, check_vma=False
    )
```

profile of v0, /device:TPU:32, one launch (start us, length us, event | category | flops | bytes accessed | tf_op | source)
XLA Modules:
  0.0 551.5 jit_solution(15502643504803332840)
XLA Ops:
  2.9 3.8 copy.234
  9.2 4.6 collective-permute-start.1
  14.4 5.1 collective-permute-start.5
  20.8 34.8 %reshape.153 = f32[16,2,16,2,64,2]{5,4,3,2,1,0:T(8,128)} reshape(f32[32,32,128]{2,1,0:T(8,128)S(1)} %copy.236) | data formatting | bytes 1048576 | tf_op jit(solution)/shard_map/reshape | solution.py:76
  55.6 12.2 %reduce_sum.119 = f32[16,16,64]{2,1,0:T(8,128)S(1)} reduce(f32[16,2,16,2,64,2]{5,4,3,2,1,0:T(8,128)} %reshape.153, f32[]{:T(128)} %constant.37.clone.1), dimensions={1,3,5}, to_apply=%region_2.3 | reduce | flops 114688 | bytes 589828 | tf_op jit(solution)/shard_map/reduce_sum | solution.py:76
  67.8 5.7 %mul.494 = f32[8,2,8,2,32,2]{5,4,3,2,1,0:T(8,128)} reshape(f32[16,16,64]{2,1,0:T(8,128)S(1)} %broadcast_multiply_fusion) | data formatting | bytes 131072 | tf_op jit(solution)/shard_map/mul | solution.py:187
  73.5 2.6 reduce_sum.121
  78.4 2.7 fusion.150
  81.1 2.7 fusion.151
  83.8 2.5 fusion.149
  104.8 3.8 collective-permute-start.6
  108.6 2.0 collective-permute-start.7
  110.7 2.0 collective-permute-start.4
  112.7 3.8 collective-permute-start.2
  116.5 2.0 collective-permute-start.3
  119.1 3.8 copy.233
  127.9 7.9 %fusion.41 = f32[32,32,128]{1,0,2:T(8,128)S(1)} fusion(f32[1,32,128]{1,0,2:T(1,128)} %collective-permute-done.7, f32[1,32,128]{1,0,2:T(1,128)S(1)} %collective-permute-done.6, f32[32,32,1]{1,0,2:T(8,128)} %collective-permute-done.4, f32[32,32,128]{1,0,2:T(8,128)} %copy.233, f32[32]{0:T(128)} %pad_multiply_fusion.2, f32[128]{0:T(128)} %concatenate.274, ...), kind=kLoop, calls=%fused_computation.72 | loop fusion | flops 5636096 | bytes 3744640 | tf_op jit(solution)/shard_map/jit(_where)/select_n | solution.py:177
  136.6 2.1 fusion.146
  138.7 5.1 collective-permute-start.9
  143.9 4.9 collective-permute-start.10
  148.8 15.3 %collective-permute-start.11 = (f32[1,32,128]{1,0,2:T(1,128)S(1)}, f32[1,32,128]{1,0,2:T(1,128)S(1)}, u32[]{:S(2)}, u32[]{:S(2)}) collective-permute-start(f32[1,32,128]{1,0,2:T(1,128)S(1)} %get-tuple-element.241), channel_id=1, source_target_pairs={{1,0},{2,1},{3,2},{4,3},{5,4},{6,5},{7,6},{9,8},{10,9},{11,10},{12... | collective-permute-start | bytes 49160 | tf_op jit(solution)/shard_map/ppermute | solution.py:25
  164.1 2.6 fusion.144
  167.4 4.8 collective-permute-start.18
  174.2 5.1 collective-permute-start.14
  181.4 8.6 %fusion.27 = f32[32,32,128]{1,0,2:T(8,128)} fusion(f32[1,32,128]{1,0,2:T(1,128)S(1)} %collective-permute-done.11, f32[32,32,128]{1,0,2:T(8,128)S(1)} %fusion.41, f32[1,32,128]{1,0,2:T(1,128)S(1)} %collective-permute-done.10, f32[32,32,127]{1,0,2:T(8,128)} %get-tuple-element.235, f32[32,32,1]{1,0,2:T(8,128)S(1)} %collective-permute-done.8, ...), kind=kLoop, calls=%fused_computation.42 | loop fusion | flops 6029312 | bytes 6357248 | tf_op jit(solution)/shard_map/jit(_where)/select_n | solution.py:181
  190.0 2.7 copy.235
  192.7 34.8 %reshape.152 = f32[16,2,16,2,64,2]{5,4,3,2,1,0:T(8,128)} reshape(f32[32,32,128]{2,1,0:T(8,128)S(1)} %copy.235) | data formatting | bytes 1048576 | tf_op jit(solution)/shard_map/reshape | solution.py:76
  227.5 12.3 %reduce_sum.118 = f32[16,16,64]{2,1,0:T(8,128)S(1)} reduce(f32[16,2,16,2,64,2]{5,4,3,2,1,0:T(8,128)} %reshape.152, f32[]{:T(128)} %constant.37.clone.1), dimensions={1,3,5}, to_apply=%region_1.2 | reduce | flops 114688 | bytes 589828 | tf_op jit(solution)/shard_map/reduce_sum | solution.py:76
  244.2 5.0 collective-permute-start.21
  249.2 5.0 collective-permute-start.22
  258.4 5.1 collective-permute-start.30
  265.5 5.1 collective-permute-start.26
  274.1 5.7 %reshape.154 = f32[8,2,8,2,32,2]{5,4,3,2,1,0:T(8,128)} reshape(f32[16,16,64]{2,1,0:T(8,128)S(1)} %fusion.69) | data formatting | bytes 131072 | tf_op jit(solution)/shard_map/reshape | solution.py:76
  279.9 2.6 reduce_sum.120
  284.3 4.6 collective-permute-start.33
  288.8 5.1 collective-permute-start.34
  296.0 4.4 collective-permute-done.35
  301.7 79.6 %all-gather = f32[512,4,4,16]{3,2,1,0:T(4,128)S(1)} all-gather(f32[2,4,4,16]{3,2,1,0:T(4,128)S(1)} %pad_maximum_fusion.18), channel_id=2, replica_groups=mesh['box'=32,'sub'=8] {'box','sub'}, dimensions={0}, use_global_device_ids=true | all-gather | bytes 526336 | tf_op jit(solution)/shard_map/all_gather | solution.py:150
  382.7 3.3 copy.239
  386.0 4.9 reshape.159
  392.6 4.0 gather_fusion
  400.1 3.8 fusion.47
  416.1 63.4 %while.17 = (s32[]{:T(128)}, f32[32,4,256]{2,1,0:T(4,128)}, f32[32,4,256]{2,1,0:T(4,128)}, f32[32,4,256]{2,1,0:T(4,128)S(1)}, f32[]{:T(128)}, /*index=5*/f32[32,...) while((s32[]{:T(128)}, f32[32,4,256]{2,1,0:T(4,128)}, ...), condition=%wide.region_14.15_spmd.clone, body=%wide.region_11.14_spmd.clone.sunk | while | flops 950275 | bytes 4825283 | solution.py:140
  419.6 2.2 multiply_reduce_fusion.5
  426.8 2.2 multiply_reduce_fusion.5
  434.8 2.2 multiply_reduce_fusion.5
  442.9 2.2 multiply_reduce_fusion.5
  450.9 2.2 multiply_reduce_fusion.5
  458.9 2.2 multiply_reduce_fusion.5
  467.0 2.2 multiply_reduce_fusion.5
  475.0 2.2 multiply_reduce_fusion.5
  482.2 2.0 collective-permute-start.37
  484.2 3.0 collective-permute-start.38
  487.2 2.9 collective-permute-start.39
  499.1 3.9 collective-permute-start.41
  503.0 3.6 collective-permute-start.42
  506.7 2.9 collective-permute-start.43
  521.1 4.2 collective-permute-start.46
  525.3 2.5 collective-permute-start.47
  527.9 3.4 collective-permute-start.45
  531.4 2.8 fusion.139
  534.2 3.7 collective-permute-done.44
  538.5 9.3 %fusion.42 = f32[32,32,128]{1,0,2:T(8,128)} fusion(f32[32,32,128]{1,0,2:T(8,128)S(1)} %bitcast_add_fusion, f32[1,32,128]{1,0,2:T(1,128)} %collective-permute-done.47, f32[1,32,128]{1,0,2:T(1,128)} %collective-permute-done.46, f32[32,1,128]{1,0,2:T(8,128)S(1)} %get-tuple-element.227, f32[32,31,128]{1,0,2:T(8,128)S(1)} %get-tuple-element.229, ...), kind=kLoop, calls=%fused_computation.73 | loop fusion | flops 6422528 | bytes 6357248 | tf_op jit(solution)/shard_map/jit(_where)/select_n | solution.py:177
  547.9 3.4 copy.261
  (400 shorter events, 127.3 us)
Async XLA Ops:
  9.2 101.5 %collective-permute-start.1 = (f32[32,32,1]{1,0,2:T(8,128)}, f32[32,32,1]{1,0,2:T(8,128)S(1)}, u32[]{:S(2)}, u32[]{:S(2)}) collective-permute-start(f32[32,32,1]{1,0,2:T(8,128)} %get-tuple-element.242), channel_id=1, source_target_pairs={{8,0},{16,8},{24,16},{32,24},{40,32},{48,40},{56,48},{64,56},{72,6... | collective-permute-start | bytes 12296 | tf_op jit(solution)/shard_map/ppermute | solution.py:25
  13.8 98.8 %collective-permute-start = (f32[32,32,1]{1,0,2:T(8,128)}, f32[32,32,1]{1,0,2:T(8,128)S(1)}, u32[]{:S(2)}, u32[]{:S(2)}) collective-permute-start(f32[32,32,1]{1,0,2:T(8,128)} %get-tuple-element.243), channel_id=1, source_target_pairs={{0,8},{8,16},{16,24},{24,32},{32,40},{40,48},{48,56},{56,64},{64,7... | collective-permute-start | bytes 12296 | tf_op jit(solution)/shard_map/ppermute | solution.py:22
  14.4 102.1 %collective-permute-start.5 = (f32[32,32,1]{1,0,2:T(8,128)}, f32[32,32,1]{1,0,2:T(8,128)}, u32[]{:S(2)}, u32[]{:S(2)}) collective-permute-start(f32[32,32,1]{1,0,2:T(8,128)} %broadcast.217), channel_id=1, source_target_pairs={{8,0},{16,8},{24,16},{32,24},{40,32},{48,40},{56,48},{64,56},{72,6... | collective-permute-start | bytes 12296 | tf_op jit(solution)/shard_map/ppermute | solution.py:25
  76.1 224.3 %copy-start.15 = (f32[8,8,32]{2,1,0:T(8,128)}, f32[8,8,32]{2,1,0:T(8,128)S(1)}, u32[]{:S(2)}) copy-start(f32[8,8,32]{2,1,0:T(8,128)S(1)} %broadcast_multiply_fusion.1) | copy-start | bytes 24580
  77.4 23.9 %collective-permute-start.25 = (f32[8,8,1]{2,1,0:T(8,128)}, f32[8,8,1]{2,1,0:T(8,128)S(1)}, u32[]{:S(2)}, u32[]{:S(2)}) collective-permute-start(f32[8,8,1]{2,1,0:T(8,128)} %get-tuple-element.315), channel_id=1, source_target_pairs={{8,0},{16,8},{24,16},{32,24},{40,32},{48,40},{56,48},{64,56},{72,6... | collective-permute-start | bytes 776 | tf_op jit(solution)/shard_map/ppermute | solution.py:25
  78.1 23.3 %collective-permute-start.29 = (f32[8,8,1]{2,1,0:T(8,128)}, f32[8,8,1]{2,1,0:T(8,128)}, u32[]{:S(2)}, u32[]{:S(2)}) collective-permute-start(f32[8,8,1]{2,1,0:T(8,128)} %broadcast.228), channel_id=1, source_target_pairs={{8,0},{16,8},{24,16},{32,24},{40,32},{48,40},{56,48},{64,56},{72,6... | collective-permute-start | bytes 776 | tf_op jit(solution)/shard_map/ppermute | solution.py:25
  88.3 184.3 %copy-start.19 = (f32[16,16,63]{2,1,0:T(8,128)}, f32[16,16,63]{2,1,0:T(8,128)S(1)}, u32[]{:S(2)}) copy-start(f32[16,16,63]{2,1,0:T(8,128)S(1)} %get-tuple-element.287) | copy-start | bytes 193540
  88.3 184.3 %copy-start.21 = (f32[16,15,64]{2,1,0:T(8,128)}, f32[16,15,64]{2,1,0:T(8,128)S(1)}, u32[]{:S(2)}) copy-start(f32[16,15,64]{2,1,0:T(8,128)S(1)} %get-tuple-element.290) | copy-start | bytes 184324
  88.3 184.3 %copy-start.23 = (f32[16,15,64]{2,1,0:T(8,128)}, f32[16,15,64]{2,1,0:T(8,128)S(1)}, u32[]{:S(2)}) copy-start(f32[16,15,64]{2,1,0:T(8,128)S(1)} %get-tuple-element.291) | copy-start | bytes 184324
  92.0 208.4 %copy-start.31 = (f32[8,8,31]{2,1,0:T(8,128)}, f32[8,8,31]{2,1,0:T(8,128)S(1)}, u32[]{:S(2)}) copy-start(f32[8,8,31]{2,1,0:T(8,128)S(1)} %get-tuple-element.317) | copy-start | bytes 23812
  92.0 208.4 %copy-start.32 = (f32[8,7,32]{2,1,0:T(8,128)}, f32[8,7,32]{2,1,0:T(8,128)S(1)}, u32[]{:S(2)}) copy-start(f32[8,7,32]{2,1,0:T(8,128)S(1)} %get-tuple-element.320) | copy-start | bytes 21508
  92.0 208.4 %copy-start.33 = (f32[8,7,32]{2,1,0:T(8,128)}, f32[8,7,32]{2,1,0:T(8,128)S(1)}, u32[]{:S(2)}) copy-start(f32[8,7,32]{2,1,0:T(8,128)S(1)} %get-tuple-element.321) | copy-start | bytes 21508
  101.3 2.8 collective-permute-start.13
  102.0 6.6 %collective-permute-start.17 = (f32[16,16,1]{2,1,0:T(8,128)}, f32[16,16,1]{2,1,0:T(8,128)S(1)}, u32[]{:S(2)}, u32[]{:S(2)}) collective-permute-start(f32[16,16,1]{2,1,0:T(8,128)} %broadcast.223), channel_id=1, source_target_pairs={{8,0},{16,8},{24,16},{32,24},{40,32},{48,40},{56,48},{64,56},{72,6... | collective-permute-start | bytes 3080 | tf_op jit(solution)/shard_map/ppermute | solution.py:25
  104.8 23.0 %collective-permute-start.6 = (f32[1,32,128]{1,0,2:T(1,128)}, f32[1,32,128]{1,0,2:T(1,128)S(1)}, u32[]{:S(2)}, u32[]{:S(2)}) collective-permute-start(f32[1,32,128]{1,0,2:T(1,128)} %broadcast.219), channel_id=1, source_target_pairs={{0,1},{1,2},{2,3},{3,4},{4,5},{5,6},{6,7},{8,9},{9,10},{10,11},{11... | collective-permute-start | bytes 49160 | tf_op jit(solution)/shard_map/ppermute | solution.py:22
  108.6 19.2 %collective-permute-start.7 = (f32[1,32,128]{1,0,2:T(1,128)}, f32[1,32,128]{1,0,2:T(1,128)}, u32[]{:S(2)}, u32[]{:S(2)}) collective-permute-start(f32[1,32,128]{1,0,2:T(1,128)} %broadcast.219), channel_id=1, source_target_pairs={{1,0},{2,1},{3,2},{4,3},{5,4},{6,5},{7,6},{9,8},{10,9},{11,10},{12... | collective-permute-start | bytes 49160 | tf_op jit(solution)/shard_map/ppermute | solution.py:25
  110.7 70.6 %copy-start.36 = (f32[32,32,1]{1,0,2:T(8,128)}, f32[32,32,1]{1,0,2:T(8,128)S(1)}, u32[]{:S(2)}) copy-start(f32[32,32,1]{1,0,2:T(8,128)S(1)} %collective-permute-done.1) | copy-start | bytes 12292
  110.7 17.1 %collective-permute-start.4 = (f32[32,32,1]{1,0,2:T(8,128)}, f32[32,32,1]{1,0,2:T(8,128)}, u32[]{:S(2)}, u32[]{:S(2)}) collective-permute-start(f32[32,32,1]{1,0,2:T(8,128)} %broadcast.217), channel_id=1, source_target_pairs={{0,8},{8,16},{16,24},{24,32},{32,40},{40,48},{48,56},{56,64},{64,7... | collective-permute-start | bytes 12296 | tf_op jit(solution)/shard_map/ppermute | solution.py:22
  112.7 68.6 %copy-start.37 = (f32[32,32,1]{1,0,2:T(8,128)}, f32[32,32,1]{1,0,2:T(8,128)S(1)}, u32[]{:S(2)}) copy-start(f32[32,32,1]{1,0,2:T(8,128)S(1)} %collective-permute-done) | copy-start | bytes 12292
  112.7 15.1 %collective-permute-start.2 = (f32[1,32,128]{1,0,2:T(1,128)}, f32[1,32,128]{1,0,2:T(1,128)S(1)}, u32[]{:S(2)}, u32[]{:S(2)}) collective-permute-start(f32[1,32,128]{1,0,2:T(1,128)} %get-tuple-element.251), channel_id=1, source_target_pairs={{0,1},{1,2},{2,3},{3,4},{4,5},{5,6},{6,7},{8,9},{9,10},{10,11},{11... | collective-permute-start | bytes 49160 | tf_op jit(solution)/shard_map/ppermute | solution.py:22
  116.5 11.3 %collective-permute-start.3 = (f32[1,32,128]{1,0,2:T(1,128)}, f32[1,32,128]{1,0,2:T(1,128)S(1)}, u32[]{:S(2)}, u32[]{:S(2)}) collective-permute-start(f32[1,32,128]{1,0,2:T(1,128)} %get-tuple-element.250), channel_id=1, source_target_pairs={{1,0},{2,1},{3,2},{4,3},{5,4},{6,5},{7,6},{9,8},{10,9},{11,10},{12... | collective-permute-start | bytes 49160 | tf_op jit(solution)/shard_map/ppermute | solution.py:25
  127.8 38.9 %collective-permute-start.12 = (f32[16,16,1]{2,1,0:T(8,128)S(1)}, f32[16,16,1]{2,1,0:T(8,128)S(1)}, u32[]{:S(2)}, u32[]{:S(2)}) collective-permute-start(f32[16,16,1]{2,1,0:T(8,128)S(1)} %copy-done.39), channel_id=1, source_target_pairs={{0,8},{8,16},{16,24},{24,32},{32,40},{40,48},{48,56},{56,64},{64,7... | collective-permute-start | bytes 3080 | tf_op jit(solution)/shard_map/ppermute | solution.py:22
  127.8 53.5 %copy-start.26 = (f32[1,32,128]{1,0,2:T(1,128)}, f32[1,32,128]{1,0,2:T(1,128)S(1)}, u32[]{:S(2)}) copy-start(f32[1,32,128]{1,0,2:T(1,128)S(1)} %collective-permute-done.2) | copy-start | bytes 49156
  127.8 53.5 %copy-start.28 = (f32[1,32,128]{1,0,2:T(1,128)}, f32[1,32,128]{1,0,2:T(1,128)S(1)}, u32[]{:S(2)}) copy-start(f32[1,32,128]{1,0,2:T(1,128)S(1)} %collective-permute-done.3) | copy-start | bytes 49156
  135.8 45.5 %copy-start = (f32[32,32,128]{1,0,2:T(8,128)}, f32[32,32,128]{1,0,2:T(8,128)S(1)}, u32[]{:S(2)}) copy-start(f32[32,32,128]{1,0,2:T(8,128)S(1)} %fusion.41) | copy-start | bytes 1572868
  136.5 44.8 %copy-start.7 = (f32[32,31,128]{1,0,2:T(8,128)S(1)}, f32[32,31,128]{1,0,2:T(8,128)}, u32[]{:S(2)}) copy-start(f32[32,31,128]{1,0,2:T(8,128)} %get-tuple-element.248) | copy-start | bytes 1523716
  138.7 28.0 %collective-permute-start.9 = (f32[32,32,1]{1,0,2:T(8,128)S(1)}, f32[32,32,1]{1,0,2:T(8,128)S(1)}, u32[]{:S(2)}, u32[]{:S(2)}) collective-permute-start(f32[32,32,1]{1,0,2:T(8,128)S(1)} %get-tuple-element.232), channel_id=1, source_target_pairs={{8,0},{16,8},{24,16},{32,24},{40,32},{48,40},{56,48},{64,56},{72,6... | collective-permute-start | bytes 12296 | tf_op jit(solution)/shard_map/ppermute | solution.py:25
  143.9 28.4 %collective-permute-start.8 = (f32[32,32,1]{1,0,2:T(8,128)S(1)}, f32[32,32,1]{1,0,2:T(8,128)S(1)}, u32[]{:S(2)}, u32[]{:S(2)}) collective-permute-start(f32[32,32,1]{1,0,2:T(8,128)S(1)} %get-tuple-element.233), channel_id=1, source_target_pairs={{0,8},{8,16},{16,24},{24,32},{32,40},{40,48},{48,56},{56,64},{64,7... | collective-permute-start | bytes 12296 | tf_op jit(solution)/shard_map/ppermute | solution.py:22
  143.9 30.3 %collective-permute-start.10 = (f32[1,32,128]{1,0,2:T(1,128)S(1)}, f32[1,32,128]{1,0,2:T(1,128)S(1)}, u32[]{:S(2)}, u32[]{:S(2)}) collective-permute-start(f32[1,32,128]{1,0,2:T(1,128)S(1)} %get-tuple-element.240), channel_id=1, source_target_pairs={{0,1},{1,2},{2,3},{3,4},{4,5},{5,6},{6,7},{8,9},{9,10},{10,11},{11... | collective-permute-start | bytes 49160 | tf_op jit(solution)/shard_map/ppermute | solution.py:22
  148.8 30.5 %collective-permute-start.11 = (f32[1,32,128]{1,0,2:T(1,128)S(1)}, f32[1,32,128]{1,0,2:T(1,128)S(1)}, u32[]{:S(2)}, u32[]{:S(2)}) collective-permute-start(f32[1,32,128]{1,0,2:T(1,128)S(1)} %get-tuple-element.241), channel_id=1, source_target_pairs={{1,0},{2,1},{3,2},{4,3},{5,4},{6,5},{7,6},{9,8},{10,9},{11,10},{12... | collective-permute-start | bytes 49160 | tf_op jit(solution)/shard_map/ppermute | solution.py:25
  166.7 73.1 %collective-permute-start.16 = (f32[16,16,1]{2,1,0:T(8,128)}, f32[16,16,1]{2,1,0:T(8,128)}, u32[]{:S(2)}, u32[]{:S(2)}) collective-permute-start(f32[16,16,1]{2,1,0:T(8,128)} %broadcast.223), channel_id=1, source_target_pairs={{0,8},{8,16},{16,24},{24,32},{32,40},{40,48},{48,56},{56,64},{64,7... | collective-permute-start | bytes 3080 | tf_op jit(solution)/shard_map/ppermute | solution.py:22
  167.4 72.6 %collective-permute-start.18 = (f32[1,16,64]{2,1,0:T(8,128)}, f32[1,16,64]{2,1,0:T(8,128)}, u32[]{:S(2)}, u32[]{:S(2)}) collective-permute-start(f32[1,16,64]{2,1,0:T(8,128)} %broadcast.224), channel_id=1, source_target_pairs={{0,1},{1,2},{2,3},{3,4},{4,5},{5,6},{6,7},{8,9},{9,10},{10,11},{11... | collective-permute-start | bytes 12296 | tf_op jit(solution)/shard_map/ppermute | solution.py:22
  172.2 67.7 %collective-permute-start.19 = (f32[1,16,64]{2,1,0:T(8,128)}, f32[1,16,64]{2,1,0:T(8,128)}, u32[]{:S(2)}, u32[]{:S(2)}) collective-permute-start(f32[1,16,64]{2,1,0:T(8,128)} %broadcast.224), channel_id=1, source_target_pairs={{1,0},{2,1},{3,2},{4,3},{5,4},{6,5},{7,6},{9,8},{10,9},{11,10},{12... | collective-permute-start | bytes 12296 | tf_op jit(solution)/shard_map/ppermute | solution.py:25
  174.2 65.7 %collective-permute-start.14 = (f32[1,16,64]{2,1,0:T(8,128)}, f32[1,16,64]{2,1,0:T(8,128)}, u32[]{:S(2)}, u32[]{:S(2)}) collective-permute-start(f32[1,16,64]{2,1,0:T(8,128)} %get-tuple-element.293), channel_id=1, source_target_pairs={{0,1},{1,2},{2,3},{3,4},{4,5},{5,6},{6,7},{8,9},{9,10},{10,11},{11... | collective-permute-start | bytes 12296 | tf_op jit(solution)/shard_map/ppermute | solution.py:22
  179.3 60.6 %collective-permute-start.15 = (f32[1,16,64]{2,1,0:T(8,128)}, f32[1,16,64]{2,1,0:T(8,128)}, u32[]{:S(2)}, u32[]{:S(2)}) collective-permute-start(f32[1,16,64]{2,1,0:T(8,128)} %get-tuple-element.292), channel_id=1, source_target_pairs={{1,0},{2,1},{3,2},{4,3},{5,4},{6,5},{7,6},{9,8},{10,9},{11,10},{12... | collective-permute-start | bytes 12296 | tf_op jit(solution)/shard_map/ppermute | solution.py:25
  239.8 18.0 %collective-permute-start.24 = (f32[8,8,1]{2,1,0:T(8,128)S(1)}, f32[8,8,1]{2,1,0:T(8,128)S(1)}, u32[]{:S(2)}, u32[]{:S(2)}) collective-permute-start(f32[8,8,1]{2,1,0:T(8,128)S(1)} %copy-done.55), channel_id=1, source_target_pairs={{0,8},{8,16},{16,24},{24,32},{32,40},{40,48},{48,56},{56,64},{64,7... | collective-permute-start | bytes 776 | tf_op jit(solution)/shard_map/ppermute | solution.py:22
  244.2 12.0 %collective-permute-start.21 = (f32[16,16,1]{2,1,0:T(8,128)S(1)}, f32[16,16,1]{2,1,0:T(8,128)S(1)}, u32[]{:S(2)}, u32[]{:S(2)}) collective-permute-start(f32[16,16,1]{2,1,0:T(8,128)S(1)} %get-tuple-element.274), channel_id=1, source_target_pairs={{8,0},{16,8},{24,16},{32,24},{40,32},{48,40},{56,48},{64,56},{72,6... | collective-permute-start | bytes 3080 | tf_op jit(solution)/shard_map/ppermute | solution.py:25
  249.2 14.4 %collective-permute-start.20 = (f32[16,16,1]{2,1,0:T(8,128)}, f32[16,16,1]{2,1,0:T(8,128)S(1)}, u32[]{:S(2)}, u32[]{:S(2)}) collective-permute-start(f32[16,16,1]{2,1,0:T(8,128)} %get-tuple-element.275), channel_id=1, source_target_pairs={{0,8},{8,16},{16,24},{24,32},{32,40},{40,48},{48,56},{56,64},{64,7... | collective-permute-start | bytes 3080 | tf_op jit(solution)/shard_map/ppermute | solution.py:22
  249.2 16.3 %collective-permute-start.22 = (f32[1,16,64]{2,1,0:T(8,128)}, f32[1,16,64]{2,1,0:T(8,128)}, u32[]{:S(2)}, u32[]{:S(2)}) collective-permute-start(f32[1,16,64]{2,1,0:T(8,128)} %get-tuple-element.282), channel_id=1, source_target_pairs={{0,1},{1,2},{2,3},{3,4},{4,5},{5,6},{6,7},{8,9},{9,10},{10,11},{11... | collective-permute-start | bytes 12296 | tf_op jit(solution)/shard_map/ppermute | solution.py:22
  254.2 16.5 %collective-permute-start.23 = (f32[1,16,64]{2,1,0:T(8,128)}, f32[1,16,64]{2,1,0:T(8,128)}, u32[]{:S(2)}, u32[]{:S(2)}) collective-permute-start(f32[1,16,64]{2,1,0:T(8,128)} %get-tuple-element.283), channel_id=1, source_target_pairs={{1,0},{2,1},{3,2},{4,3},{5,4},{6,5},{7,6},{9,8},{10,9},{11,10},{12... | collective-permute-start | bytes 12296 | tf_op jit(solution)/shard_map/ppermute | solution.py:25
  256.8 25.6 %collective-permute-start.28 = (f32[8,8,1]{2,1,0:T(8,128)}, f32[8,8,1]{2,1,0:T(8,128)}, u32[]{:S(2)}, u32[]{:S(2)}) collective-permute-start(f32[8,8,1]{2,1,0:T(8,128)} %broadcast.228), channel_id=1, source_target_pairs={{0,8},{8,16},{16,24},{24,32},{32,40},{40,48},{48,56},{56,64},{64,7... | collective-permute-start | bytes 776 | tf_op jit(solution)/shard_map/ppermute | solution.py:22
  258.4 24.1 %collective-permute-start.30 = (f32[1,8,32]{2,1,0:T(8,128)}, f32[1,8,32]{2,1,0:T(8,128)}, u32[]{:S(2)}, u32[]{:S(2)}) collective-permute-start(f32[1,8,32]{2,1,0:T(8,128)} %broadcast.229), channel_id=1, source_target_pairs={{0,1},{1,2},{2,3},{3,4},{4,5},{5,6},{6,7},{8,9},{9,10},{10,11},{11... | collective-permute-start | bytes 3080 | tf_op jit(solution)/shard_map/ppermute | solution.py:22
  263.6 18.9 %collective-permute-start.31 = (f32[1,8,32]{2,1,0:T(8,128)}, f32[1,8,32]{2,1,0:T(8,128)}, u32[]{:S(2)}, u32[]{:S(2)}) collective-permute-start(f32[1,8,32]{2,1,0:T(8,128)} %broadcast.229), channel_id=1, source_target_pairs={{1,0},{2,1},{3,2},{4,3},{5,4},{6,5},{7,6},{9,8},{10,9},{11,10},{12... | collective-permute-start | bytes 3080 | tf_op jit(solution)/shard_map/ppermute | solution.py:25
  265.5 16.9 %collective-permute-start.26 = (f32[1,8,32]{2,1,0:T(8,128)}, f32[1,8,32]{2,1,0:T(8,128)S(1)}, u32[]{:S(2)}, u32[]{:S(2)}) collective-permute-start(f32[1,8,32]{2,1,0:T(8,128)} %get-tuple-element.323), channel_id=1, source_target_pairs={{0,1},{1,2},{2,3},{3,4},{4,5},{5,6},{6,7},{8,9},{9,10},{10,11},{11... | collective-permute-start | bytes 3080 | tf_op jit(solution)/shard_map/ppermute | solution.py:22
  270.7 11.8 %collective-permute-start.27 = (f32[1,8,32]{2,1,0:T(8,128)}, f32[1,8,32]{2,1,0:T(8,128)S(1)}, u32[]{:S(2)}, u32[]{:S(2)}) collective-permute-start(f32[1,8,32]{2,1,0:T(8,128)} %get-tuple-element.322), channel_id=1, source_target_pairs={{1,0},{2,1},{3,2},{4,3},{5,4},{6,5},{7,6},{9,8},{10,9},{11,10},{12... | collective-permute-start | bytes 3080 | tf_op jit(solution)/shard_map/ppermute | solution.py:25
  282.4 98.9 %copy-start.30 = (f32[8,8,32]{2,1,0:T(8,128)}, f32[8,8,32]{2,1,0:T(8,128)S(1)}, u32[]{:S(2)}) copy-start(f32[8,8,32]{2,1,0:T(8,128)S(1)} %reduce_sum.120) | copy-start | bytes 24580
  284.1 97.2 %copy-start.16 = (f32[8,8,32]{2,1,0:T(8,128)}, f32[8,8,32]{2,1,0:T(8,128)S(1)}, u32[]{:S(2)}) copy-start(f32[8,8,32]{2,1,0:T(8,128)S(1)} %get-tuple-element.206) | copy-start | bytes 24580
  284.1 97.2 %copy-start.35 = (f32[8,8,32]{2,1,0:T(8,128)}, f32[8,8,32]{2,1,0:T(8,128)S(1)}, u32[]{:S(2)}) copy-start(f32[8,8,32]{2,1,0:T(8,128)S(1)} %get-tuple-element.207) | copy-start | bytes 24580
  284.3 11.7 %collective-permute-start.33 = (f32[8,8,1]{2,1,0:T(8,128)S(1)}, f32[8,8,1]{2,1,0:T(8,128)S(1)}, u32[]{:S(2)}, u32[]{:S(2)}) collective-permute-start(f32[8,8,1]{2,1,0:T(8,128)S(1)} %get-tuple-element.304), channel_id=1, source_target_pairs={{8,0},{16,8},{24,16},{32,24},{40,32},{48,40},{56,48},{64,56},{72,6... | collective-permute-start | bytes 776 | tf_op jit(solution)/shard_map/ppermute | solution.py:25
  288.8 7.2 %collective-permute-start.32 = (f32[8,8,1]{2,1,0:T(8,128)S(1)}, f32[8,8,1]{2,1,0:T(8,128)S(1)}, u32[]{:S(2)}, u32[]{:S(2)}) collective-permute-start(f32[8,8,1]{2,1,0:T(8,128)S(1)} %get-tuple-element.305), channel_id=1, source_target_pairs={{0,8},{8,16},{16,24},{24,32},{32,40},{40,48},{48,56},{56,64},{64,7... | collective-permute-start | bytes 776 | tf_op jit(solution)/shard_map/ppermute | solution.py:22
  288.8 7.2 %collective-permute-start.34 = (f32[1,8,32]{2,1,0:T(8,128)S(1)}, f32[1,8,32]{2,1,0:T(8,128)S(1)}, u32[]{:S(2)}, u32[]{:S(2)}) collective-permute-start(f32[1,8,32]{2,1,0:T(8,128)S(1)} %get-tuple-element.312), channel_id=1, source_target_pairs={{0,1},{1,2},{2,3},{3,4},{4,5},{5,6},{6,7},{8,9},{9,10},{10,11},{11... | collective-permute-start | bytes 3080 | tf_op jit(solution)/shard_map/ppermute | solution.py:22
  294.0 6.4 %collective-permute-start.35 = (f32[1,8,32]{2,1,0:T(8,128)S(1)}, f32[1,8,32]{2,1,0:T(8,128)S(1)}, u32[]{:S(2)}, u32[]{:S(2)}) collective-permute-start(f32[1,8,32]{2,1,0:T(8,128)S(1)} %get-tuple-element.313), channel_id=1, source_target_pairs={{1,0},{2,1},{3,2},{4,3},{5,4},{6,5},{7,6},{9,8},{10,9},{11,10},{12... | collective-permute-start | bytes 3080 | tf_op jit(solution)/shard_map/ppermute | solution.py:25
  482.2 7.9 %collective-permute-start.37 = (f32[8,8,1]{2,1,0:T(8,128)S(1)}, f32[8,8,1]{2,1,0:T(8,128)S(1)}, u32[]{:S(2)}, u32[]{:S(2)}) collective-permute-start(f32[8,8,1]{2,1,0:T(8,128)S(1)} %get-tuple-element.294), channel_id=1, source_target_pairs={{8,0},{16,8},{24,16},{32,24},{40,32},{48,40},{56,48},{64,56},{72,6... | collective-permute-start | bytes 776 | tf_op jit(solution)/shard_map/ppermute | solution.py:25
  484.2 6.7 %collective-permute-start.36 = (f32[8,8,1]{2,1,0:T(8,128)S(1)}, f32[8,8,1]{2,1,0:T(8,128)S(1)}, u32[]{:S(2)}, u32[]{:S(2)}) collective-permute-start(f32[8,8,1]{2,1,0:T(8,128)S(1)} %get-tuple-element.295), channel_id=1, source_target_pairs={{0,8},{8,16},{16,24},{24,32},{32,40},{40,48},{48,56},{56,64},{64,7... | collective-permute-start | bytes 776 | tf_op jit(solution)/shard_map/ppermute | solution.py:22
  484.2 6.7 %collective-permute-start.38 = (f32[1,8,32]{2,1,0:T(8,128)S(1)}, f32[1,8,32]{2,1,0:T(8,128)S(1)}, u32[]{:S(2)}, u32[]{:S(2)}) collective-permute-start(f32[1,8,32]{2,1,0:T(8,128)S(1)} %get-tuple-element.302), channel_id=1, source_target_pairs={{0,1},{1,2},{2,3},{3,4},{4,5},{5,6},{6,7},{8,9},{9,10},{10,11},{11... | collective-permute-start | bytes 3080 | tf_op jit(solution)/shard_map/ppermute | solution.py:22
  487.2 5.7 %collective-permute-start.39 = (f32[1,8,32]{2,1,0:T(8,128)S(1)}, f32[1,8,32]{2,1,0:T(8,128)S(1)}, u32[]{:S(2)}, u32[]{:S(2)}) collective-permute-start(f32[1,8,32]{2,1,0:T(8,128)S(1)} %get-tuple-element.303), channel_id=1, source_target_pairs={{1,0},{2,1},{3,2},{4,3},{5,4},{6,5},{7,6},{9,8},{10,9},{11,10},{12... | collective-permute-start | bytes 3080 | tf_op jit(solution)/shard_map/ppermute | solution.py:25
  499.1 11.1 %collective-permute-start.41 = (f32[16,16,1]{2,1,0:T(8,128)S(1)}, f32[16,16,1]{2,1,0:T(8,128)}, u32[]{:S(2)}, u32[]{:S(2)}) collective-permute-start(f32[16,16,1]{2,1,0:T(8,128)S(1)} %get-tuple-element.264), channel_id=1, source_target_pairs={{8,0},{16,8},{24,16},{32,24},{40,32},{48,40},{56,48},{64,56},{72,6... | collective-permute-start | bytes 3080 | tf_op jit(solution)/shard_map/ppermute | solution.py:25
  503.0 8.8 %collective-permute-start.40 = (f32[16,16,1]{2,1,0:T(8,128)}, f32[16,16,1]{2,1,0:T(8,128)S(1)}, u32[]{:S(2)}, u32[]{:S(2)}) collective-permute-start(f32[16,16,1]{2,1,0:T(8,128)} %get-tuple-element.265), channel_id=1, source_target_pairs={{0,8},{8,16},{16,24},{24,32},{32,40},{40,48},{48,56},{56,64},{64,7... | collective-permute-start | bytes 3080 | tf_op jit(solution)/shard_map/ppermute | solution.py:22
  503.0 8.8 %collective-permute-start.42 = (f32[1,16,64]{2,1,0:T(8,128)}, f32[1,16,64]{2,1,0:T(8,128)}, u32[]{:S(2)}, u32[]{:S(2)}) collective-permute-start(f32[1,16,64]{2,1,0:T(8,128)} %get-tuple-element.272), channel_id=1, source_target_pairs={{0,1},{1,2},{2,3},{3,4},{4,5},{5,6},{6,7},{8,9},{9,10},{10,11},{11... | collective-permute-start | bytes 12296 | tf_op jit(solution)/shard_map/ppermute | solution.py:22
  506.7 6.4 %collective-permute-start.43 = (f32[1,16,64]{2,1,0:T(8,128)}, f32[1,16,64]{2,1,0:T(8,128)}, u32[]{:S(2)}, u32[]{:S(2)}) collective-permute-start(f32[1,16,64]{2,1,0:T(8,128)} %get-tuple-element.273), channel_id=1, source_target_pairs={{1,0},{2,1},{3,2},{4,3},{5,4},{6,5},{7,6},{9,8},{10,9},{11,10},{12... | collective-permute-start | bytes 12296 | tf_op jit(solution)/shard_map/ppermute | solution.py:25
  521.1 16.8 %collective-permute-start.46 = (f32[1,32,128]{1,0,2:T(1,128)S(1)}, f32[1,32,128]{1,0,2:T(1,128)}, u32[]{:S(2)}, u32[]{:S(2)}) collective-permute-start(f32[1,32,128]{1,0,2:T(1,128)S(1)} %get-tuple-element.230), channel_id=1, source_target_pairs={{0,1},{1,2},{2,3},{3,4},{4,5},{5,6},{6,7},{8,9},{9,10},{10,11},{11... | collective-permute-start | bytes 49160 | tf_op jit(solution)/shard_map/ppermute | solution.py:22
  525.3 12.6 %collective-permute-start.47 = (f32[1,32,128]{1,0,2:T(1,128)S(1)}, f32[1,32,128]{1,0,2:T(1,128)}, u32[]{:S(2)}, u32[]{:S(2)}) collective-permute-start(f32[1,32,128]{1,0,2:T(1,128)S(1)} %get-tuple-element.231), channel_id=1, source_target_pairs={{1,0},{2,1},{3,2},{4,3},{5,4},{6,5},{7,6},{9,8},{10,9},{11,10},{12... | collective-permute-start | bytes 49160 | tf_op jit(solution)/shard_map/ppermute | solution.py:25
  527.9 6.4 %collective-permute-start.45 = (f32[32,32,1]{1,0,2:T(8,128)S(1)}, f32[32,32,1]{1,0,2:T(8,128)S(1)}, u32[]{:S(2)}, u32[]{:S(2)}) collective-permute-start(f32[32,32,1]{1,0,2:T(8,128)S(1)} %get-tuple-element.222), channel_id=1, source_target_pairs={{8,0},{16,8},{24,16},{32,24},{40,32},{48,40},{56,48},{64,56},{72,6... | collective-permute-start | bytes 12296 | tf_op jit(solution)/shard_map/ppermute | solution.py:25
  531.3 6.6 %collective-permute-start.44 = (f32[32,32,1]{1,0,2:T(8,128)S(1)}, f32[32,32,1]{1,0,2:T(8,128)S(1)}, u32[]{:S(2)}, u32[]{:S(2)}) collective-permute-start(f32[32,32,1]{1,0,2:T(8,128)S(1)} %get-tuple-element.223), channel_id=1, source_target_pairs={{0,8},{8,16},{16,24},{24,32},{32,40},{40,48},{48,56},{56,64},{64,7... | collective-permute-start | bytes 12296 | tf_op jit(solution)/shard_map/ppermute | solution.py:22
  (53 other events, 782.6 us)
where the time goes:
time: 561 us; the launch traced here: 551 us
  local copies, waits for them, and re-layouts  173 us (31%)
  other arithmetic  137 us (24%)
  starting transfers between devices  129 us (23%)
  blocking collectives  79.6 us (14%)
  loops' own time  15.1 us (3%)
  waiting for transfers between devices  13 us (2%)
    all_gather x1, blocking collectives, coarse_level(): gathered = lax.all_gather(stacked[None], ('box', 'sub'), axis=0, tiled=True)  79.6 us
    reshape x4, local copies, waits for them, and re-layouts, children_sum(): field.reshape(plane_count // 2, 2, row_count // 2, 2, col_count // 2, 2)  75.6 us
    ppermute x24, starting transfers between devices, padded_2(): lax.ppermute(lax.slice_in_dim(block, 0, width, axis=dim), axis, backward)  73.4 us
    ppermute x24, starting transfers between devices, padded_2(): lax.ppermute(lax.slice_in_dim(block, block.shape[dim] - width, None, axis...  55.8 us
    reduce_sum x17, other arithmetic, local_total(): return jnp.sum(values)  36.4 us
    reduce_sum x6, other arithmetic, children_sum(): field.reshape(plane_count // 2, 2, row_count // 2, 2, col_count // 2, 2)  29.8 us
    select_n x6, other arithmetic, smooth(): jnp.where(inside, relax(potential, source_level, nearby, couple, diagonal...  21.9 us
    unnamed x149, local copies, waits for them, and re-layouts  21 us
  transfers between devices with their start and end apart: 48, of which 6 were waited for; matrix products, arithmetic and copies ran while one was open for 33% of the time, Pallas kernels for 0%

commit v1 on v0

v1 whole, which is shorter than its diff:
```python
import functools
import jax
import jax.numpy as jnp
from jax import lax
from jax.experimental import pallas as pl
from jax.experimental.pallas import tpu as pltpu
from jax.sharding import PartitionSpec as P

CAP = 4
SWEEPS = 8
OMEGA = 0.8
REST = 0.2
TINY = 1e-20
F32 = jnp.float32
BF16 = jnp.bfloat16
MESH = pl.DeviceIdType.MESH


def split(x):
    high = x.astype(BF16)
    rest = x - high.astype(F32)
    middle = rest.astype(BF16)
    low = (rest - middle.astype(F32)).astype(BF16)
    return (high, middle, low)


def pick_right(x, chosen):
    return sum(jnp.dot(part, chosen, preferred_element_type=F32) for part in split(x))


def pick_left(chosen, x):
    return sum(jnp.dot(chosen, part, preferred_element_type=F32) for part in split(x))


def pick_left_t(chosen, x):
    return sum(
        lax.dot_general(chosen, part, (((1,), (1,)), ((), ())), preferred_element_type=F32)
        for part in split(x)
    )


def ones_where(mask):
    return jnp.where(mask, 1.0, 0.0).astype(BF16)


def iota(shape, dim):
    return lax.broadcasted_iota(jnp.int32, shape, dim)


def turn(x, shift, axis):
    return pltpu.roll(x, shift, axis)


def around(x, step):
    rows = x.shape[-2]
    ax, ay = x.ndim - 1, x.ndim - 2
    return (
        turn(x, step, ax) + turn(x, 128 - step, ax) + turn(x, 1, ay) + turn(x, rows - 1, ay)
    )


def kernel(
    nb, ns,
    counts, source, beta, out,
    b0, f0, u0, v0, w0, rs, xs0, xr0, e0m, e0g,
    b1, f1, u1, v1, w1, xs1b, xr1b, xs1f, xr1f, y1, e1x,
    b2, f2, u2, v2, w2, xs2b, xr2b, xs2f, xr2f, y2,
    t3, tx, xa, ga, xb, gb_all, onehot, b3, f3, d3, i3, p3, r3, s3,
    in_sem, send_sem, recv_sem, zsend, zrecv, bsend, brecv,
):
    lanes_n = 16 * ns
    nz3 = 4 * ns
    vn = nb
    me, sub = lax.axis_index("box"), lax.axis_index("sub")
    left, right = lax.rem(me + nb - 1, nb), lax.rem(me + 1, nb)
    down, up = lax.rem(sub + ns - 1, ns), lax.rem(sub + 1, ns)
    floor, roof = sub == 0, sub == ns - 1

    get_b = pltpu.make_async_copy(beta, b0.at[pl.ds(2, 32)], in_sem.at[0])
    get_f = pltpu.make_async_copy(source, f0.at[pl.ds(1, 32)], in_sem.at[1])
    get_b.start()
    get_f.start()

    barrier = pltpu.get_barrier_semaphore()

    def greet_sub(k, carry):
        pl.semaphore_signal(
            barrier, inc=1, device_id=(me, lax.rem(sub + k, ns)), device_id_type=MESH
        )
        return carry

    def greet_box(k, carry):
        pl.semaphore_signal(
            barrier, inc=1, device_id=(lax.rem(me + k, nb), sub), device_id_type=MESH
        )
        return carry

    lax.fori_loop(1, ns, greet_sub, 0)
    lax.fori_loop(1, nb, greet_box, 0)
    for there in (left, right):
        for level in (down, up):
            pl.semaphore_signal(barrier, inc=1, device_id=(there, level), device_id_type=MESH)

    width = 32 * counts[me]
    width_left = 32 * counts[left]
    half = width // 2
    half_left = width_left // 2
    kk = iota((1, nb * 16), 1)
    kd, kj = kk // 16, kk % 16

    def place(d, carry):
        where_from, begin, mine = carry
        here = counts[d]
        value = jnp.where(kj < 4 * here, 4 * begin + kj, -1)
        where_from = jnp.where(kd == d, value, where_from)
        mine = jnp.where(d == me, begin, mine)
        return where_from, begin + here, mine

    where_from, _, my_start = lax.fori_loop(
        0, nb, place, (jnp.full((1, nb * 16), -1, jnp.int32), jnp.int32(0), jnp.int32(0))
    )
    row = iota((8 * vn, nb * 16), 0)
    onehot[...] = ones_where((row % 8) * vn + row // 8 == where_from)

    lane = iota((32, 128), 1)
    live = lane < width
    edge = (lane == 0) | (lane == width - 1)
    first_lane, last_lane = lane == 0, lane == 127
    mask_b = (lane < 2) | ((lane >= width - 2) & live)
    mask_f = edge

    ll = iota((128, 128), 0)
    lc = iota((128, 128), 1)
    squeeze = ones_where((ll // 2 == lc) & (ll < width))

    get_b.wait()
    get_f.wait()

    def load_plane(z, carry):
        tb, tf = carry
        b = jnp.where(live, b0[z + 2], 0.0)
        f = jnp.where(live, f0[z + 1], 0.0)
        b0[z + 2] = b
        f0[z + 1] = f
        tb = tb + turn(jnp.where(mask_b, b, 0.0), 4 * z, 1)
        tf = tf + turn(jnp.where(mask_f, f, 0.0), 4 * z, 1)
        return tb, tf

    zero_tile = jnp.zeros((32, 128), F32)
    tb, tf = lax.fori_loop(0, 32, load_plane, (zero_tile, zero_tile))
    xs0[0] = tb
    xs0[1] = tf

    pl.semaphore_wait(barrier, (ns - 1) + (nb - 1) + 4)

    def x_copies(src, dst, base):
        made = []
        for side, there in ((0, right), (1, left)):
            for slot, level in ((0, up), (1, sub), (2, down)):
                n = base + side * 3 + slot
                made.append(
                    pltpu.make_async_remote_copy(
                        src_ref=src, dst_ref=dst.at[side, slot],
                        send_sem=send_sem.at[n], recv_sem=recv_sem.at[n],
                        device_id=(there, level), device_id_type=MESH,
                    )
                )
        return made

    def z_copies(ref, own, halo, base):
        made = []
        for n, (begin, to, level) in enumerate(
            ((own, 0, up), (halo, own + halo, down))
        ):
            made.append(
                pltpu.make_async_remote_copy(
                    src_ref=ref.at[pl.ds(begin, halo)], dst_ref=ref.at[pl.ds(to, halo)],
                    send_sem=send_sem.at[base + n], recv_sem=recv_sem.at[base + n],
                    device_id=(me, level), device_id_type=MESH,
                )
            )
        return made

    def start(copies):
        for copy in copies:
            copy.start()

    def wait(copies):
        for copy in copies:
            copy.wait()

    copies0 = x_copies(xs0, xr0, 0) + z_copies(b0, 32, 2, 6) + z_copies(f0, 32, 1, 8)
    start(copies0)

    def squeeze_level0():
        both = rs[:, pl.ds(0, 16, stride=2), :] + rs[:, pl.ds(1, 16, stride=2), :]
        return pick_right(both.reshape(256, 128), squeeze).reshape(16, 16, 128)

    def coarsen(x, scratch, step):
        planes, rows, _ = x.shape
        pairs = x.reshape(planes // 2, 2, rows, 128)
        scratch[...] = pairs[:, 0] + pairs[:, 1]
        y = (
            scratch[:, pl.ds(0, rows // 2, stride=2), :]
            + scratch[:, pl.ds(1, rows // 2, stride=2), :]
        )
        odd = (iota(y.shape, 2) // step) % 2 == 1
        return y + jnp.where(odd, turn(y, step, 2), turn(y, 128 - step, 2))

    def pack(x, tile_ref, group, reach):
        planes, rows, _ = x.shape
        at = iota((rows, 128), 1)
        keep = (at < reach) | ((at >= half - reach) & (at < half))
        total = jnp.zeros((rows, 128), F32)
        for z in range(planes):
            total = total + turn(jnp.where(keep, x[z], 0.0), group * z, 1)
        tile_ref[...] = total

    def to_slots(x):
        for z in range(4):
            t3[pl.ds(z, 4, stride=8), :] = x[z]
            t3[pl.ds(z + 4, 4, stride=8), :] = x[z]
        tiles = t3[...].reshape(4, 1, 8, 128)
        tiles = jnp.broadcast_to(tiles, (4, ns // 2, 8, 128)).reshape(lanes_n, 128)
        tx[...] = jnp.transpose(tiles)
        return tx[pl.ds(0, 16, stride=4), :]

    def sub_copy(k, which, slot):
        return pltpu.make_async_remote_copy(
            src_ref=xa.at[which], dst_ref=ga.at[which, slot],
            send_sem=zsend.at[which, k], recv_sem=zrecv.at[which, k],
            device_id=(me, lax.rem(sub + k, ns)), device_id_type=MESH,
        )

    def box_copy(k, which, slot):
        return pltpu.make_async_remote_copy(
            src_ref=xb.at[which], dst_ref=gb_all.at[which, slot],
            send_sem=bsend.at[which, k], recv_sem=brecv.at[which, k],
            device_id=(lax.rem(me + k, nb), sub), device_id_type=MESH,
        )

    def send_all(make, which, mine, count):
        def body(k, carry):
            make(k, which, mine).start()
            return carry
        lax.fori_loop(1, count, body, 0)

    def wait_all(make, which, mine, count):
        def body(k, carry):
            copy = make(k, which, lax.rem(mine - k + count, count))
            copy.wait_send()
            copy.wait_recv()
            return carry
        lax.fori_loop(1, count, body, 0)

    def gather_start(x, which):
        tile = to_slots(x)
        xa[which] = tile
        ga[which, sub] = tile
        send_all(sub_copy, which, sub, ns)

    def gather_turn(which):
        wait_all(sub_copy, which, sub, ns)
        at = (iota((16, lanes_n), 1) // 4) % ns
        tile = jnp.zeros((16, lanes_n), F32)
        for k in range(ns):
            tile = jnp.where(at == k, ga[which, k], tile)
        xb[which] = tile
        gb_all[which, me] = tile
        send_all(box_copy, which, me, nb)

    def gather_end(which):
        wait_all(box_copy, which, me, nb)
        rows = gb_all[which].reshape(nb * 16, lanes_n)
        return pick_left(onehot[...], rows).reshape(vn, 8, lanes_n)

    def pair_b(k, carry):
        rs[k] = b0[2 * k + 2] + b0[2 * k + 3]
        return carry

    lax.fori_loop(0, 16, pair_b, 0)
    own_b1 = 0.125 * squeeze_level0()
    b1[pl.ds(3, 16)] = own_b1
    pack(own_b1, xs1b, 8, 3)
    copies_b1 = x_copies(xs1b, xr1b, 10) + z_copies(b1, 16, 3, 16)
    start(copies_b1)
    own_b2 = 0.125 * coarsen(own_b1, y1, 1)
    b2[pl.ds(3, 8)] = own_b2
    pack(own_b2, xs2b, 16, 6)
    copies_b2 = x_copies(xs2b, xr2b, 18) + z_copies(b2, 8, 3, 24)
    start(copies_b2)
    gather_start(0.125 * coarsen(own_b2, y2, 2), 0)

    wait(copies0)

    @pl.when(floor)
    def _():
        b0[pl.ds(0, 2)] = jnp.zeros((2, 32, 128), F32)
        f0[pl.ds(0, 1)] = jnp.zeros((1, 32, 128), F32)

    @pl.when(roof)
    def _():
        b0[pl.ds(34, 2)] = jnp.zeros((2, 32, 128), F32)
        f0[pl.ds(33, 1)] = jnp.zeros((1, 32, 128), F32)

    quarter = lane % 4
    group = lane // 4
    q0, q3 = quarter == 0, quarter == 3
    turn_l1 = lax.rem(129 - width_left + 128, 128)
    turn_l2 = lax.rem(130 - width_left + 128, 128)

    def ghost(slot, which, near_by):
        from_left, from_right = xr0[0, slot, which], xr0[1, slot, which]
        shift_l = turn_l1 if near_by == 1 else turn_l2
        return jnp.where(
            q0, turn(from_left, shift_l, 1),
            jnp.where(q3, turn(from_right, lax.rem(width - near_by, 128), 1), 0.0),
        )

    ghost_b = ghost(1, 0, 1)
    ghost_b_low = jnp.where(floor, 0.0, ghost(0, 0, 1))
    ghost_b_high = jnp.where(roof, 0.0, ghost(2, 0, 1))
    ghost_b_far = ghost(1, 0, 2)
    ghost_f = ghost(1, 1, 1)
    own_edge = jnp.where(q0 | q3, tb, 0.0)
    turned = width // 4 - 1
    first_z = (q0 & (group == 0)) | (q3 & (group == turned))
    last_z = (q0 & (group == 31)) | (q3 & (group == lax.rem(31 + turned, 32)))
    ghost_sum = (
        ghost_b_far + own_edge + turn(ghost_b, 1, 0) + turn(ghost_b, 31, 0)
        + turn(jnp.where(first_z, ghost_b_high, ghost_b), 124, 1)
        + turn(jnp.where(last_z, ghost_b_low, ghost_b), 4, 1)
    )
    ghost_diag = 3.0 * ghost_b + 0.5 * ghost_sum
    ghost_u = OMEGA * ghost_f / jnp.maximum(ghost_diag, TINY)
    ghost_k = ghost_b + own_edge
    ghost_c = ghost_k * ghost_u

    def spread(v):
        return (
            turn(jnp.where(last_lane, 0.0, v), 1, 1) + turn(jnp.where(first_lane, 0.0, v), 127, 1)
            + turn(v, 1, 0) + turn(v, 31, 0)
        )

    def start_plane(e, tile, shift):
        b = b0[e + 1]
        f = f0[e]
        total = spread(b) + b0[e] + b0[e + 2] + jnp.where(edge, turn(tile, shift, 1), 0.0)
        w = OMEGA / jnp.maximum(3.0 * b + 0.5 * total, TINY)
        u = w * f
        w0[e] = w
        u0[e] = u
        v0[e] = b * u

    def start_own(z, carry):
        start_plane(z + 1, ghost_b, lax.rem(128 - 4 * z, 128))
        return carry

    lax.fori_loop(0, 32, start_own, 0)
    start_plane(0, ghost_b_low, 4)
    start_plane(33, ghost_b_high, 0)

    def pull(e):
        return b0[e + 1] * (spread(u0[e]) + u0[e - 1] + u0[e + 1]) + (
            spread(v0[e]) + v0[e - 1] + v0[e + 1]
        )

    def residual(z):
        gain = pull(z + 1) + jnp.where(edge, turn(ghost_c, lax.rem(128 - 4 * z, 128), 1), 0.0)
        return REST * f0[z + 1] + 0.5 * gain

    def pair_r(k, carry):
        rs[k] = residual(2 * k) + residual(2 * k + 1)
        return carry

    lax.fori_loop(0, 16, pair_r, 0)

    def join(ref, xr, own, halo, gr, reach):
        rows = ref.shape[1]
        at = iota((rows, 128), 1)
        inside = at < half
        keep = ((at >= half) & (at < half + reach)) | (at >= 128 - reach)
        sub_at = at % gr
        tiles = []
        for slot in range(3):
            from_left = turn(xr[0, slot], lax.rem(256 - half_left, 128), 1)
            from_right = turn(xr[1, slot], half, 1)
            tiles.append(
                jnp.where(
                    sub_at >= gr - reach, from_left, jnp.where(sub_at < reach, from_right, 0.0)
                )
            )
        for z in range(-halo, own + halo):
            slot = 0 if z < 0 else (2 if z >= own else 1)
            there = z % own
            plane = jnp.where(
                inside, ref[z + halo],
                jnp.where(keep, turn(tiles[slot], (128 - gr * there) % 128, 1), 0.0),
            )
            if z < 0:
                plane = jnp.where(floor, 0.0, plane)
            if z >= own:
                plane = jnp.where(roof, 0.0, plane)
            ref[z + halo] = plane

    def weights(b, step):
        n = b.shape[0]
        middle = b[1:n - 1]
        total = around(middle, step) + b[:n - 2] + b[2:]
        return OMEGA / jnp.maximum(3.0 * middle + 0.5 * total, TINY)

    def gain_of(b, u, v, step):
        n = u.shape[0]
        return b * (around(u[1:n - 1], step) + u[:n - 2] + u[2:]) + (
            around(v[1:n - 1], step) + v[:n - 2] + v[2:]
        )

    def begin_level(b_ref, f_ref, w_ref, u_ref, v_ref, own, step):
        w = w_ref[...]
        u = w * f_ref[...]
        u_ref[...] = u
        v = b_ref[pl.ds(1, own + 4)] * u
        v_ref[...] = v
        b = b_ref[pl.ds(3, own)]
        gain = gain_of(b, u[1:own + 3], v[1:own + 3], step)
        return REST * f_ref[pl.ds(2, own)] + 0.5 * gain

    def end_level(b_ref, f_ref, w_ref, u, own, step):
        v = b_ref[pl.ds(1, own + 4)] * u
        b = b_ref[pl.ds(2, own + 2)]
        gain = gain_of(b, u, v, step)
        e = REST * u[1:own + 3] + w_ref[pl.ds(1, own + 2)] * (
            f_ref[pl.ds(1, own + 2)] + 0.5 * gain
        )
        return jnp.concatenate([
            jnp.where(floor, 0.0, e[:1]), e[1:own + 1], jnp.where(roof, 0.0, e[own + 1:])
        ], 0)

    own_f1 = 0.5 * squeeze_level0()
    f1[pl.ds(2, 16)] = own_f1
    pack(own_f1, xs1f, 8, 2)
    copies_f1 = x_copies(xs1f, xr1f, 26) + z_copies(f1, 16, 2, 32)
    start(copies_f1)

    gather_turn(0)
    wait(copies_b1)
    join(b1, xr1b, 16, 3, 8, 3)
    w1[...] = weights(b1[...], 1)

    wait(copies_f1)
    join(f1, xr1f, 16, 2, 8, 2)
    r1 = begin_level(b1, f1, w1, u1, v1, 16, 1)
    own_f2 = 0.5 * coarsen(r1, y1, 1)
    own_f2 = jnp.where(iota(own_f2.shape, 2) < half, own_f2, 0.0)
    f2[pl.ds(2, 8)] = own_f2
    pack(own_f2, xs2f, 16, 4)
    copies_f2 = x_copies(xs2f, xr2f, 34) + z_copies(f2, 8, 2, 40)
    start(copies_f2)

    wait(copies_b2)
    join(b2, xr2b, 8, 3, 16, 6)
    w2[...] = weights(b2[...], 2)

    wait(copies_f2)
    join(f2, xr2f, 8, 2, 16, 4)
    r2 = begin_level(b2, f2, w2, u2, v2, 8, 2)
    gather_start(0.5 * coarsen(r2, y2, 2), 1)
    gather_turn(1)

    zz = iota((vn, 8, lanes_n), 2) % nz3
    not_top, not_bottom = zz < nz3 - 1, zz > 0

    def around3(p):
        return (
            jnp.concatenate([p[1:], turn(p[:1], 7, 1)], 0)
            + jnp.concatenate([turn(p[vn - 1:], 1, 1), p[:vn - 1]], 0)
            + turn(p, nz3, 2) + turn(p, lanes_n - nz3, 2)
            + jnp.where(not_top, turn(p, lanes_n - 1, 2), 0.0)
            + jnp.where(not_bottom, turn(p, 1, 2), 0.0)
        )

    def total3(x):
        tile = jnp.sum(x, axis=0)
        return jnp.sum(jnp.sum(tile, axis=0, keepdims=True), axis=1, keepdims=True)

    coarse_b = gather_end(0)
    b3[...] = coarse_b
    coarse_d = 3.0 * coarse_b + 0.5 * around3(coarse_b)
    d3[...] = coarse_d
    i3[...] = 1.0 / coarse_d

    coarse_f = gather_end(1)
    r3[...] = coarse_f
    first_p = coarse_f * i3[...]
    p3[...] = first_p
    s3[...] = jnp.zeros((vn, 8, lanes_n), F32)

    def iterate(n, rz):
        p = p3[...]
        b = b3[...]
        q = d3[...] * p - 0.5 * (b * around3(p) + around3(b * p))
        alpha = rz / total3(p * q)
        s3[...] = s3[...] + alpha * p
        r = r3[...] - alpha * q
        r3[...] = r
        scaled = r * i3[...]
        new = total3(r * scaled)
        p3[...] = scaled + (new / rz) * p
        return new

    lax.fori_loop(0, SWEEPS, iterate, total3(coarse_f * first_p))

    l_at, k_at = iota((128, 8 * vn), 0), iota((128, 8 * vn), 1)
    relative = jnp.where(l_at < 124, l_at // 4, -1)
    wanted = lax.rem(4 * my_start + relative + 8 * vn, 8 * vn)
    from_x = ones_where((k_at % 8) * vn + k_at // 8 == wanted)
    by_lane = pick_left(from_x, s3[...].reshape(8 * vn, lanes_n))
    q_at, r_at = iota((48, lanes_n), 0), iota((48, lanes_n), 1)
    z_at = 4 * sub + q_at // 8 - 1
    from_row = ones_where(
        (r_at == ((q_at % 8) // 2) * nz3 + z_at) & (z_at >= 0) & (z_at < nz3)
    )
    e3 = pick_left_t(from_row, by_lane).reshape(6, 1, 8, 128)
    e3 = jnp.broadcast_to(e3, (6, 2, 8, 128)).reshape(12, 8, 128)

    e2 = end_level(b2, f2, w2, u2[...] + e3, 8, 2)
    e1x[:, pl.ds(0, 8, stride=2), :] = e2
    e1x[:, pl.ds(1, 8, stride=2), :] = e2
    grown = jnp.broadcast_to(e1x[...].reshape(10, 1, 16, 128), (10, 2, 16, 128))
    e1 = end_level(b1, f1, w1, u1[...] + grown.reshape(20, 16, 128), 16, 1)

    si, sc = iota((128, 256), 0), iota((128, 256), 1)
    stretch = ones_where(
        ((sc < width) & (si == sc // 2))
        | ((sc == 128) & (si == 127))
        | ((sc == 128 + width - 1) & (si == half))
    )
    wide = pick_right(e1.reshape(288, 128), stretch)
    main = wide[:, :128].reshape(18, 16, 128)
    side = wide[:, 128:].reshape(18, 16, 128)
    e0m[:, pl.ds(0, 16, stride=2), :] = main
    e0m[:, pl.ds(1, 16, stride=2), :] = main
    e0g[:, pl.ds(0, 16, stride=2), :] = side
    e0g[:, pl.ds(1, 16, stride=2), :] = side

    def add_plane(e, carry):
        u = u0[e] + e0m[(e + 1) // 2]
        u0[e] = u
        v0[e] = b0[e + 1] * u
        return carry

    lax.fori_loop(0, 34, add_plane, 0)

    def finish(z, carry):
        shift = lax.rem(128 - 4 * z, 128)
        ends = jnp.where(edge, turn(ghost_c, shift, 1), 0.0)
        ends = ends + turn(ghost_k, shift, 1) * e0g[z // 2 + 1]
        gain = pull(z + 1) + ends
        u = REST * u0[z + 1] + w0[z + 1] * (f0[z + 1] + 0.5 * gain)
        out[z] = jnp.where(live, u, 0.0)
        return carry

    lax.fori_loop(0, 32, finish, 0)


def per_device(nb, ns, source, beta, counts):
    lanes_n = 16 * ns

    def vmem(*shape, dtype=F32):
        return pltpu.VMEM(shape, dtype)

    def coarse():
        return vmem(nb, 8, lanes_n)

    scratch = [
        vmem(36, 32, 128), vmem(34, 32, 128), vmem(34, 32, 128), vmem(34, 32, 128),
        vmem(34, 32, 128), vmem(16, 32, 128), vmem(2, 32, 128), vmem(2, 3, 2, 32, 128),
        vmem(18, 32, 128), vmem(18, 32, 128),
        vmem(22, 16, 128), vmem(20, 16, 128), vmem(20, 16, 128), vmem(20, 16, 128),
        vmem(20, 16, 128), vmem(16, 128), vmem(2, 3, 16, 128), vmem(16, 128), vmem(2, 3, 16, 128), vmem(8, 16, 128),
        vmem(10, 16, 128),
        vmem(14, 8, 128), vmem(12, 8, 128), vmem(12, 8, 128), vmem(12, 8, 128),
        vmem(12, 8, 128), vmem(8, 128), vmem(2, 3, 8, 128), vmem(8, 128), vmem(2, 3, 8, 128), vmem(4, 8, 128),
        vmem(32, 128), vmem(128, lanes_n), vmem(2, 16, lanes_n), vmem(2, ns, 16, lanes_n),
        vmem(2, 16, lanes_n), vmem(2, nb, 16, lanes_n), vmem(8 * nb, 16 * nb, dtype=BF16),
        coarse(), coarse(), coarse(), coarse(), coarse(), coarse(), coarse(),
        pltpu.SemaphoreType.DMA((2,)),
        pltpu.SemaphoreType.DMA((42,)), pltpu.SemaphoreType.DMA((42,)),
        pltpu.SemaphoreType.DMA((2, ns)), pltpu.SemaphoreType.DMA((2, ns)),
        pltpu.SemaphoreType.DMA((2, nb)), pltpu.SemaphoreType.DMA((2, nb)),
    ]
    return pl.pallas_call(
        functools.partial(kernel, nb, ns),
        out_shape=jax.ShapeDtypeStruct(source.shape, F32),
        in_specs=[
            pl.BlockSpec(memory_space=pltpu.SMEM),
            pl.BlockSpec(memory_space=pl.ANY),
            pl.BlockSpec(memory_space=pl.ANY),
        ],
        out_specs=pl.BlockSpec(memory_space=pltpu.VMEM),
        scratch_shapes=scratch,
        compiler_params=pltpu.CompilerParams(
            collective_id=0, has_side_effects=True, vmem_limit_bytes=32 * 1024 * 1024
        ),
    )(counts, source, beta)


def solution(mesh):
    in_specs = (P("sub", None, "box"), P("sub", None, "box"), P())
    out_specs = P("sub", None, "box")
    return jax.shard_map(
        functools.partial(per_device, mesh.shape["box"], mesh.shape["sub"]),
        mesh=mesh, in_specs=in_specs, out_specs=out_specs, check_vma=False,
    )
```

time: 561 us -> 58.9 us (0.10)
  the two profiles are of different devices: /device:TPU:32 before, /device:TPU:1 now
where the time goes in v1:
time: 58.9 us; the launch traced here: 58.7 us
  Pallas kernels  55.1 us (94%)
  local copies, waits for them, and re-layouts  3.53 us (6%)
    pallas_call x1, Pallas kernels, per_device(): pl.pallas_call(functools.partial(kernel, nb, ns), out_shape=jax.ShapeDtyp...  55.1 us
    unnamed x7, local copies, waits for them, and re-layouts  3.53 us

profile of v1, /device:TPU:1, one launch (start us, length us, event | category | flops | bytes accessed | tf_op | source)
XLA Modules:
  0.0 58.7 jit_solution(15698606229999541097)
XLA Ops:
  0.0 0.0 copy-start
  0.0 1.0 %copy-done = f32[32,32,128]{2,1,0:T(8,128)S(1)} copy-done((f32[32,32,128]{2,1,0:T(8,128)S(1)}, f32[32,32,128]{2,1,0:T(8,128)}, u32[]{:S(2)}) %copy-start) | copy-done | bytes 524312
  1.0 0.0 copy-start.1
  1.0 1.0 %copy-done.1 = f32[32,32,128]{2,1,0:T(8,128)S(1)} copy-done((f32[32,32,128]{2,1,0:T(8,128)S(1)}, f32[32,32,128]{2,1,0:T(8,128)}, u32[]{:S(2)}) %copy-start.1) | copy-done | bytes 524312
  2.1 0.0 copy-start.2
  2.1 0.7 %copy-done.2 = s32[32]{0:T(128)S(1)} copy-done((s32[32]{0:T(128)S(1)}, s32[32]{0:T(128)}, u32[]{:S(2)}) %copy-start.2) | copy-done | bytes 152
  2.7 55.1 %shard_map.37 = f32[32,32,128]{2,1,0:T(8,128)S(1)} custom-call(s32[32]{0:T(128)S(1)} %copy-done.2, f32[32,32,128]{2,1,0:T(8,128)S(1)} %copy-done, f32[32,32,128]{2,1,0:T(8,128)S(1)} %copy-done.1), custom_call_target="tpu_custom_call" | custom-call | tf_op jit(solution)/shard_map/pallas_call | solution.py:592
  57.9 0.8 %copy.5 = f32[32,32,128]{2,1,0:T(8,128)} copy(f32[32,32,128]{2,1,0:T(8,128)S(1)} %shard_map.37) | data formatting | bytes 1048576
Async XLA Ops:
  0.0 1.0 %copy-start = (f32[32,32,128]{2,1,0:T(8,128)S(1)}, f32[32,32,128]{2,1,0:T(8,128)}, u32[]{:S(2)}) copy-start(f32[32,32,128]{2,1,0:T(8,128)} %source.1) | copy-start | bytes 1572868
  1.0 1.0 %copy-start.1 = (f32[32,32,128]{2,1,0:T(8,128)S(1)}, f32[32,32,128]{2,1,0:T(8,128)}, u32[]{:S(2)}) copy-start(f32[32,32,128]{2,1,0:T(8,128)} %beta.1) | copy-start | bytes 1572868
  2.1 0.7 %copy-start.2 = (s32[32]{0:T(128)S(1)}, s32[32]{0:T(128)}, u32[]{:S(2)}) copy-start(s32[32]{0:T(128)} %counts.1) | copy-start | bytes 388

commit v2 on v1

--- a/solution.py
+++ b/solution.py
@@ -62,10 +62,10 @@
 def kernel(
     nb, ns,
     counts, source, beta, out,
-    b0, f0, u0, v0, w0, rs, xs0, xr0, e0m, e0g,
+    b0, f0, u0, w0, r0, kx, ky, rs, xs0, xr0, e0m, e0x, e0y, c0, cx, cy, cz,
     b1, f1, u1, v1, w1, xs1b, xr1b, xs1f, xr1f, y1, e1x,
     b2, f2, u2, v2, w2, xs2b, xr2b, xs2f, xr2f, y2,
-    t3, tx, xa, ga, xb, gb_all, onehot, b3, f3, d3, i3, p3, r3, s3,
+    t3, tx, xa, ga, xb, gb_all, onehot, kx3, ky3, kz3, d3, i3, p3, r3, s3,
     in_sem, send_sem, recv_sem, zsend, zrecv, bsend, brecv,
 ):
     lanes_n = 16 * ns
@@ -125,9 +125,8 @@
     lane = iota((32, 128), 1)
     live = lane < width
     edge = (lane == 0) | (lane == width - 1)
-    first_lane, last_lane = lane == 0, lane == 127
-    mask_b = (lane < 2) | ((lane >= width - 2) & live)
-    mask_f = edge
+    edge_two = (lane < 2) | ((lane >= width - 2) & live)
+    inner = lane < width - 1
 
     ll = iota((128, 128), 0)
     lc = iota((128, 128), 1)
@@ -136,20 +135,104 @@
     get_b.wait()
     get_f.wait()
 
-    def load_plane(z, carry):
+    def each(count, first, last, act):
+        def body(n, carry):
+            for k in range(count):
+                act(first + n * count + k)
+            return carry
+        lax.fori_loop(0, (last - first) // count, body, 0)
+
+    def load_planes(n, carry):
         tb, tf = carry
-        b = jnp.where(live, b0[z + 2], 0.0)
-        f = jnp.where(live, f0[z + 1], 0.0)
-        b0[z + 2] = b
-        f0[z + 1] = f
-        tb = tb + turn(jnp.where(mask_b, b, 0.0), 4 * z, 1)
-        tf = tf + turn(jnp.where(mask_f, f, 0.0), 4 * z, 1)
+        for k in range(4):
+            z = 4 * n + k
+            b = jnp.where(live, b0[z + 2], 0.0)
+            f = jnp.where(live, f0[z + 1], 0.0)
+            b0[z + 2] = b
+            f0[z + 1] = f
+            tb = tb + turn(jnp.where(edge_two, b, 0.0), 4 * z, 1)
+            tf = tf + turn(jnp.where(edge, f, 0.0), 4 * z, 1)
         return tb, tf
 
     zero_tile = jnp.zeros((32, 128), F32)
-    tb, tf = lax.fori_loop(0, 32, load_plane, (zero_tile, zero_tile))
+    tb, tf = lax.fori_loop(0, 8, load_planes, (zero_tile, zero_tile))
     xs0[0] = tb
     xs0[1] = tf
+
+
+    def squeeze_level0():
+        both = rs[:, pl.ds(0, 16, stride=2), :] + rs[:, pl.ds(1, 16, stride=2), :]
+        return pick_right(both.reshape(256, 128), squeeze).reshape(16, 16, 128)
+
+    def coarsen(x, scratch, step):
+        planes, rows, _ = x.shape
+        pairs = x.reshape(planes // 2, 2, rows, 128)
+        scratch[...] = pairs[:, 0] + pairs[:, 1]
+        y = (
+            scratch[:, pl.ds(0, rows // 2, stride=2), :]
+            + scratch[:, pl.ds(1, rows // 2, stride=2), :]
+        )
+        odd = (iota(y.shape, 2) // step) % 2 == 1
+        return y + jnp.where(odd, turn(y, step, 2), turn(y, 128 - step, 2))
+
+    def pack(x, tile_ref, group, reach):
+        planes, rows, _ = x.shape
+        at = iota((rows, 128), 1)
+        keep = (at < reach) | ((at >= half - reach) & (at < half))
+        total = jnp.zeros((rows, 128), F32)
+        for z in range(planes):
+            total = total + turn(jnp.where(keep, x[z], 0.0), group * z, 1)
+        tile_ref[...] = total
+
+    def to_slots(x):
+        for z in range(4):
+            t3[pl.ds(z, 4, stride=8), :] = x[z]
+            t3[pl.ds(z + 4, 4, stride=8), :] = x[z]
+        tiles = t3[...].reshape(4, 1, 8, 128)
+        tiles = jnp.broadcast_to(tiles, (4, ns // 2, 8, 128)).reshape(lanes_n, 128)
+        tx[...] = jnp.transpose(tiles)
+        return tx[pl.ds(0, 16, stride=4), :]
+
+    def pair_b(k):
+        rs[k] = b0[2 * k + 2] + b0[2 * k + 3]
+
+    each(4, 0, 16, pair_b)
+    own_b1 = 0.125 * squeeze_level0()
+    b1[pl.ds(3, 16)] = own_b1
+    pack(own_b1, xs1b, 8, 3)
+    own_b2 = 0.125 * coarsen(own_b1, y1, 1)
+    b2[pl.ds(3, 8)] = own_b2
+    pack(own_b2, xs2b, 16, 6)
+
+    def couple(e):
+        b = b0[e + 1]
+        px = jnp.where(inner, b + turn(b, 127, 1), 0.0)
+        py = b + turn(b, 31, 0)
+        kx[e] = px
+        ky[e] = py
+        return px + turn(px, 1, 1) + py + turn(py, 1, 0) + (b0[e] + b) + (b + b0[e + 2])
+
+    def start_plane(e, more=0.0):
+        w = (2.0 * OMEGA) / jnp.maximum(couple(e) + more, TINY)
+        w0[e] = w
+        u0[e] = w * f0[e]
+
+    def pull(e):
+        u, px, py, b = u0[e], kx[e], ky[e], b0[e + 1]
+        return (
+            px * turn(u, 127, 1) + turn(px * u, 1, 1) + py * turn(u, 31, 0) + turn(py * u, 1, 0)
+            + (b0[e] + b) * u0[e - 1] + (b + b0[e + 2]) * u0[e + 1]
+        )
+
+    def residual(z):
+        r = REST * f0[z + 1] + 0.5 * pull(z + 1)
+        r0[z] = r
+        return r
+
+    def pair_r(k):
+        rs[k] = residual(2 * k) + residual(2 * k + 1)
+
+    each(5, 2, 32, start_plane)
 
     pl.semaphore_wait(barrier, (ns - 1) + (nb - 1) + 4)
 
@@ -192,39 +275,6 @@
     copies0 = x_copies(xs0, xr0, 0) + z_copies(b0, 32, 2, 6) + z_copies(f0, 32, 1, 8)
     start(copies0)
 
-    def squeeze_level0():
-        both = rs[:, pl.ds(0, 16, stride=2), :] + rs[:, pl.ds(1, 16, stride=2), :]
-        return pick_right(both.reshape(256, 128), squeeze).reshape(16, 16, 128)
-
-    def coarsen(x, scratch, step):
-        planes, rows, _ = x.shape
-        pairs = x.reshape(planes // 2, 2, rows, 128)
-        scratch[...] = pairs[:, 0] + pairs[:, 1]
-        y = (
-            scratch[:, pl.ds(0, rows // 2, stride=2), :]
-            + scratch[:, pl.ds(1, rows // 2, stride=2), :]
-        )
-        odd = (iota(y.shape, 2) // step) % 2 == 1
-        return y + jnp.where(odd, turn(y, step, 2), turn(y, 128 - step, 2))
-
-    def pack(x, tile_ref, group, reach):
-        planes, rows, _ = x.shape
-        at = iota((rows, 128), 1)
-        keep = (at < reach) | ((at >= half - reach) & (at < half))
-        total = jnp.zeros((rows, 128), F32)
-        for z in range(planes):
-            total = total + turn(jnp.where(keep, x[z], 0.0), group * z, 1)
-        tile_ref[...] = total
-
-    def to_slots(x):
-        for z in range(4):
-            t3[pl.ds(z, 4, stride=8), :] = x[z]
-            t3[pl.ds(z + 4, 4, stride=8), :] = x[z]
-        tiles = t3[...].reshape(4, 1, 8, 128)
-        tiles = jnp.broadcast_to(tiles, (4, ns // 2, 8, 128)).reshape(lanes_n, 128)
-        tx[...] = jnp.transpose(tiles)
-        return tx[pl.ds(0, 16, stride=4), :]
-
     def sub_copy(k, which, slot):
         return pltpu.make_async_remote_copy(
             src_ref=xa.at[which], dst_ref=ga.at[which, slot],
@@ -274,23 +324,13 @@
         rows = gb_all[which].reshape(nb * 16, lanes_n)
         return pick_left(onehot[...], rows).reshape(vn, 8, lanes_n)
 
-    def pair_b(k, carry):
-        rs[k] = b0[2 * k + 2] + b0[2 * k + 3]
-        return carry
-
-    lax.fori_loop(0, 16, pair_b, 0)
-    own_b1 = 0.125 * squeeze_level0()
-    b1[pl.ds(3, 16)] = own_b1
-    pack(own_b1, xs1b, 8, 3)
     copies_b1 = x_copies(xs1b, xr1b, 10) + z_copies(b1, 16, 3, 16)
     start(copies_b1)
-    own_b2 = 0.125 * coarsen(own_b1, y1, 1)
-    b2[pl.ds(3, 8)] = own_b2
-    pack(own_b2, xs2b, 16, 6)
     copies_b2 = x_copies(xs2b, xr2b, 18) + z_copies(b2, 8, 3, 24)
     start(copies_b2)
     gather_start(0.125 * coarsen(own_b2, y2, 2), 0)
 
+    each(2, 1, 15, pair_r)
     wait(copies0)
 
     @pl.when(floor)
@@ -326,54 +366,55 @@
     turned = width // 4 - 1
     first_z = (q0 & (group == 0)) | (q3 & (group == turned))
     last_z = (q0 & (group == 31)) | (q3 & (group == lax.rem(31 + turned, 32)))
-    ghost_sum = (
-        ghost_b_far + own_edge + turn(ghost_b, 1, 0) + turn(ghost_b, 31, 0)
-        + turn(jnp.where(first_z, ghost_b_high, ghost_b), 124, 1)
-        + turn(jnp.where(last_z, ghost_b_low, ghost_b), 4, 1)
-    )
-    ghost_diag = 3.0 * ghost_b + 0.5 * ghost_sum
-    ghost_u = OMEGA * ghost_f / jnp.maximum(ghost_diag, TINY)
+
+    def beside(tile, low, high):
+        return (
+            turn(tile, 1, 0) + turn(tile, 31, 0)
+            + turn(jnp.where(first_z, high, tile), 124, 1)
+            + turn(jnp.where(last_z, low, tile), 4, 1)
+        )
+
     ghost_k = ghost_b + own_edge
-    ghost_c = ghost_k * ghost_u
-
-    def spread(v):
-        return (
-            turn(jnp.where(last_lane, 0.0, v), 1, 1) + turn(jnp.where(first_lane, 0.0, v), 127, 1)
-            + turn(v, 1, 0) + turn(v, 31, 0)
-        )
-
-    def start_plane(e, tile, shift):
-        b = b0[e + 1]
-        f = f0[e]
-        total = spread(b) + b0[e] + b0[e + 2] + jnp.where(edge, turn(tile, shift, 1), 0.0)
-        w = OMEGA / jnp.maximum(3.0 * b + 0.5 * total, TINY)
-        u = w * f
-        w0[e] = w
-        u0[e] = u
-        v0[e] = b * u
-
-    def start_own(z, carry):
-        start_plane(z + 1, ghost_b, lax.rem(128 - 4 * z, 128))
-        return carry
-
-    lax.fori_loop(0, 32, start_own, 0)
-    start_plane(0, ghost_b_low, 4)
-    start_plane(33, ghost_b_high, 0)
-
-    def pull(e):
-        return b0[e + 1] * (spread(u0[e]) + u0[e - 1] + u0[e + 1]) + (
-            spread(v0[e]) + v0[e - 1] + v0[e + 1]
-        )
-
-    def residual(z):
-        gain = pull(z + 1) + jnp.where(edge, turn(ghost_c, lax.rem(128 - 4 * z, 128), 1), 0.0)
-        return REST * f0[z + 1] + 0.5 * gain
-
-    def pair_r(k, carry):
-        rs[k] = residual(2 * k) + residual(2 * k + 1)
-        return carry
-
-    lax.fori_loop(0, 16, pair_r, 0)
+    ghost_sum = 6.0 * ghost_b + ghost_b_far + own_edge
+    ghost_sum = ghost_sum + beside(ghost_b, ghost_b_low, ghost_b_high)
+    ghost_u = (2.0 * OMEGA) * ghost_f / jnp.maximum(ghost_sum, TINY)
+
+    below = turn(jnp.where(edge, b0[1], 0.0), 124, 1)
+    above = jnp.where(edge, b0[34], 0.0)
+    edge_part = 6.0 * own_edge + beside(own_edge, below, above)
+    edge_part = edge_part + jnp.where(q0, turn(tb, 127, 1), turn(tb, 1, 1))
+    without = (edge_part - own_edge)
+    edge_w = (2.0 * OMEGA) / jnp.maximum(without + ghost_k, TINY)
+    edge_w = jnp.where(q0 | q3, edge_w, 0.0)
+    drift = edge_w * tf - jnp.where(
+        q0 | q3, (2.0 * OMEGA) * tf / jnp.maximum(without, TINY), 0.0
+    )
+    drift_v = own_edge * drift
+    gap = own_edge * beside(drift, 0.0, 0.0) + beside(drift_v, 0.0, 0.0) + ghost_k * ghost_u
+    gap = jnp.where(
+        q0 | q3, gap,
+        jnp.where(
+            quarter == 1, (tb + turn(own_edge, 1, 1)) * turn(drift, 1, 1),
+            (tb + turn(own_edge, 127, 1)) * turn(drift, 127, 1),
+        ),
+    )
+    gap = 0.5 * gap
+    gap_pair = gap + turn(gap, 124, 1)
+
+    def back(tile, z):
+        return turn(tile, lax.rem(128 - 4 * z, 128), 1)
+
+    start_plane(0, jnp.where(edge, turn(ghost_b_low + below, 4, 1), 0.0))
+    start_plane(1)
+    start_plane(32)
+    start_plane(33, jnp.where(edge, ghost_b_high + above, 0.0))
+    pair_r(0)
+    pair_r(15)
+
+    def mend(k):
+        rs[k] = rs[k] + jnp.where(edge_two, back(gap_pair, 2 * k), 0.0)
+
+    each(4, 0, 16, mend)
 
     def join(ref, xr, own, halo, gr, reach):
         rows = ref.shape[1]
@@ -442,7 +483,30 @@
     copies_f1 = x_copies(xs1f, xr1f, 26) + z_copies(f1, 16, 2, 32)
     start(copies_f1)
 
+    def prepare(z, odd):
+        e = z + 1
+        w = jnp.where(edge, back(edge_w, z), w0[e])
+        r = r0[z] + jnp.where(edge_two, back(gap, z), 0.0)
+        out[z] = jnp.where(live, w * (f0[e] + r), 0.0)
+        px, py, b = kx[e], ky[e], b0[e + 1]
+        px_low, py_low = turn(px, 1, 1), turn(py, 1, 0)
+        pz_low, pz = b0[e] + b, b + b0[e + 2]
+        even_x, even_y = lane % 2 == 0, iota((32, 128), 0) % 2 == 0
+        rim = jnp.where(edge, back(ghost_k, z), 0.0)
+        same = jnp.where(even_x, px, px_low) + jnp.where(even_y, py, py_low)
+        same = same + (pz_low if odd else pz)
+        w = jnp.where(live, 0.5 * w, 0.0)
+        c0[z] = REST + w * same
+        cx[z] = w * (jnp.where(even_x, px_low, px) + rim)
+        cy[z] = w * jnp.where(even_y, py_low, py)
+        cz[z] = w * (pz if odd else pz_low)
+
+    def prepare_pair(k):
+        prepare(2 * k, False)
+        prepare(2 * k + 1, True)
+
     gather_turn(0)
+    each(1, 0, 8, prepare_pair)
     wait(copies_b1)
     join(b1, xr1b, 16, 3, 8, 3)
     w1[...] = weights(b1[...], 1)
@@ -457,6 +521,7 @@
     copies_f2 = x_copies(xs2f, xr2f, 34) + z_copies(f2, 8, 2, 40)
     start(copies_f2)
 
+    each(1, 8, 16, prepare_pair)
     wait(copies_b2)
     join(b2, xr2b, 8, 3, 16, 6)
     w2[...] = weights(b2[...], 2)
@@ -467,25 +532,29 @@
     gather_start(0.5 * coarsen(r2, y2, 2), 1)
     gather_turn(1)
 
-    zz = iota((vn, 8, lanes_n), 2) % nz3
-    not_top, not_bottom = zz < nz3 - 1, zz > 0
-
-    def around3(p):
-        return (
-            jnp.concatenate([p[1:], turn(p[:1], 7, 1)], 0)
-            + jnp.concatenate([turn(p[vn - 1:], 1, 1), p[:vn - 1]], 0)
-            + turn(p, nz3, 2) + turn(p, lanes_n - nz3, 2)
-            + jnp.where(not_top, turn(p, lanes_n - 1, 2), 0.0)
-            + jnp.where(not_bottom, turn(p, 1, 2), 0.0)
-        )
+    not_top = iota((vn, 8, lanes_n), 2) % nz3 < nz3 - 1
+
+    def next_x(p):
+        return jnp.concatenate([p[1:], turn(p[:1], 7, 1)], 0)
+
+    def last_x(p):
+        return jnp.concatenate([turn(p[vn - 1:], 1, 1), p[:vn - 1]], 0)
 
     def total3(x):
         tile = jnp.sum(x, axis=0)
         return jnp.sum(jnp.sum(tile, axis=0, keepdims=True), axis=1, keepdims=True)
 
     coarse_b = gather_end(0)
-    b3[...] = coarse_b
-    coarse_d = 3.0 * coarse_b + 0.5 * around3(coarse_b)
+    px = 0.5 * (coarse_b + next_x(coarse_b))
+    py = 0.5 * (coarse_b + turn(coarse_b, lanes_n - nz3, 2))
+    pz = jnp.where(not_top, 0.5 * (coarse_b + turn(coarse_b, lanes_n - 1, 2)), 0.0)
+    ends = jnp.where(
+        not_top, 0.0, 0.5 * coarse_b
+    ) + jnp.where(iota((vn, 8, lanes_n), 2) % nz3 == 0, 0.5 * coarse_b, 0.0)
+    kx3[...] = px
+    ky3[...] = py
+    kz3[...] = pz
+    coarse_d = px + last_x(px) + py + turn(py, nz3, 2) + pz + turn(pz, 1, 2) + ends
     d3[...] = coarse_d
     i3[...] = 1.0 / coarse_d
 
@@ -495,10 +564,17 @@
     p3[...] = first_p
     s3[...] = jnp.zeros((vn, 8, lanes_n), F32)
 
+    def image(p):
+        px, py, pz = kx3[...], ky3[...], kz3[...]
+        return d3[...] * p - (
+            px * next_x(p) + last_x(px * p)
+            + py * turn(p, lanes_n - nz3, 2) + turn(py * p, nz3, 2)
+            + pz * turn(p, lanes_n - 1, 2) + turn(pz * p, 1, 2)
+        )
+
     def iterate(n, rz):
         p = p3[...]
-        b = b3[...]
-        q = d3[...] * p - 0.5 * (b * around3(p) + around3(b * p))
+        q = image(p)
         alpha = rz / total3(p * q)
         s3[...] = s3[...] + alpha * p
         r = r3[...] - alpha * q
@@ -508,13 +584,15 @@
         p3[...] = scaled + (new / rz) * p
         return new
 
-    lax.fori_loop(0, SWEEPS, iterate, total3(coarse_f * first_p))
+    rz = lax.fori_loop(0, SWEEPS - 1, iterate, total3(coarse_f * first_p))
+    last_p = p3[...]
+    solved = s3[...] + (rz / total3(last_p * image(last_p))) * last_p
 
     l_at, k_at = iota((128, 8 * vn), 0), iota((128, 8 * vn), 1)
     relative = jnp.where(l_at < 124, l_at // 4, -1)
     wanted = lax.rem(4 * my_start + relative + 8 * vn, 8 * vn)
     from_x = ones_where((k_at % 8) * vn + k_at // 8 == wanted)
-    by_lane = pick_left(from_x, s3[...].reshape(8 * vn, lanes_n))
+    by_lane = pick_left(from_x, solved.reshape(8 * vn, lanes_n))
     q_at, r_at = iota((48, lanes_n), 0), iota((48, lanes_n), 1)
     z_at = 4 * sub + q_at // 8 - 1
     from_row = ones_where(
@@ -530,37 +608,28 @@
     e1 = end_level(b1, f1, w1, u1[...] + grown.reshape(20, 16, 128), 16, 1)
 
     si, sc = iota((128, 256), 0), iota((128, 256), 1)
+    sx = sc - 128
+    step = jnp.where(sx % 2 == 0, sx // 2 - 1, sx // 2 + 1)
+    step = jnp.where(step < 0, 127, step)
     stretch = ones_where(
-        ((sc < width) & (si == sc // 2))
-        | ((sc == 128) & (si == 127))
-        | ((sc == 128 + width - 1) & (si == half))
+        ((sc < width) & (si == sc // 2)) | ((sx >= 0) & (sx < width) & (si == step))
     )
     wide = pick_right(e1.reshape(288, 128), stretch)
     main = wide[:, :128].reshape(18, 16, 128)
     side = wide[:, 128:].reshape(18, 16, 128)
     e0m[:, pl.ds(0, 16, stride=2), :] = main
     e0m[:, pl.ds(1, 16, stride=2), :] = main
-    e0g[:, pl.ds(0, 16, stride=2), :] = side
-    e0g[:, pl.ds(1, 16, stride=2), :] = side
-
-    def add_plane(e, carry):
-        u = u0[e] + e0m[(e + 1) // 2]
-        u0[e] = u
-        v0[e] = b0[e + 1] * u
-        return carry
-
-    lax.fori_loop(0, 34, add_plane, 0)
-
-    def finish(z, carry):
-        shift = lax.rem(128 - 4 * z, 128)
-        ends = jnp.where(edge, turn(ghost_c, shift, 1), 0.0)
-        ends = ends + turn(ghost_k, shift, 1) * e0g[z // 2 + 1]
-        gain = pull(z + 1) + ends
-        u = REST * u0[z + 1] + w0[z + 1] * (f0[z + 1] + 0.5 * gain)
-        out[z] = jnp.where(live, u, 0.0)
-        return carry
-
-    lax.fori_loop(0, 32, finish, 0)
+    e0x[:, pl.ds(0, 16, stride=2), :] = side
+    e0x[:, pl.ds(1, 16, stride=2), :] = side
+    e0y[:, pl.ds(0, 16, stride=2), :] = turn(main, 1, 1)
+    e0y[:, pl.ds(1, 16, stride=2), :] = turn(main, 15, 1)
+
+    def finish_pair(k):
+        e, ex, ey = e0m[k + 1], e0x[k + 1], e0y[k + 1]
+        for z, ez in ((2 * k, e0m[k]), (2 * k + 1, e0m[k + 2])):
+            out[z] = out[z] + c0[z] * e + cx[z] * ex + cy[z] * ey + cz[z] * ez
+
+    each(2, 0, 16, finish_pair)
 
 
 def per_device(nb, ns, source, beta, counts):
@@ -574,8 +643,10 @@
 
     scratch = [
         vmem(36, 32, 128), vmem(34, 32, 128), vmem(34, 32, 128), vmem(34, 32, 128),
-        vmem(34, 32, 128), vmem(16, 32, 128), vmem(2, 32, 128), vmem(2, 3, 2, 32, 128),
-        vmem(18, 32, 128), vmem(18, 32, 128),
+        vmem(32, 32, 128), vmem(34, 32, 128), vmem(34, 32, 128),
+        vmem(16, 32, 128), vmem(2, 32, 128), vmem(2, 3, 2, 32, 128),
+        vmem(18, 32, 128), vmem(18, 32, 128), vmem(18, 32, 128),
+        vmem(32, 32, 128), vmem(32, 32, 128), vmem(32, 32, 128), vmem(32, 32, 128),
         vmem(22, 16, 128), vmem(20, 16, 128), vmem(20, 16, 128), vmem(20, 16, 128),
         vmem(20, 16, 128), vmem(16, 128), vmem(2, 3, 16, 128), vmem(16, 128), vmem(2, 3, 16, 128), vmem(8, 16, 128),
         vmem(10, 16, 128),
@@ -583,7 +654,7 @@
         vmem(12, 8, 128), vmem(8, 128), vmem(2, 3, 8, 128), vmem(8, 128), vmem(2, 3, 8, 128), vmem(4, 8, 128),
         vmem(32, 128), vmem(128, lanes_n), vmem(2, 16, lanes_n), vmem(2, ns, 16, lanes_n),
         vmem(2, 16, lanes_n), vmem(2, nb, 16, lanes_n), vmem(8 * nb, 16 * nb, dtype=BF16),
-        coarse(), coarse(), coarse(), coarse(), coarse(), coarse(), coarse(),
+        coarse(), coarse(), coarse(), coarse(), coarse(), coarse(), coarse(), coarse(),
         pltpu.SemaphoreType.DMA((2,)),
         pltpu.SemaphoreType.DMA((42,)), pltpu.SemaphoreType.DMA((42,)),
         pltpu.SemaphoreType.DMA((2, ns)), pltpu.SemaphoreType.DMA((2, ns)),
@@ -600,7 +671,7 @@
         out_specs=pl.BlockSpec(memory_space=pltpu.VMEM),
         scratch_shapes=scratch,
         compiler_params=pltpu.CompilerParams(
-            collective_id=0, has_side_effects=True, vmem_limit_bytes=32 * 1024 * 1024
+            collective_id=0, has_side_effects=True, vmem_limit_bytes=62 * 1024 * 1024
         ),
     )(counts, source, beta)
 

time: 58.9 us -> 49.1 us (0.83)
  Pallas kernels: 55.1 us -> 47 us
  local copies, waits for them, and re-layouts: 3.53 us -> 1.87 us
    pallas_call x1, Pallas kernels: 55.1 us -> 47 us  [per_device(): pl.pallas_call(functools.partial(kernel, nb, ns), out_shape=jax.ShapeDtyp...]
    unnamed x7 -> x1, local copies, waits for them, and re-layouts: 3.53 us -> 1.87 us
where the time goes in v2:
time: 49.1 us; the launch traced here: 48.9 us
  Pallas kernels  47 us (96%)
  local copies, waits for them, and re-layouts  1.87 us (4%)
    pallas_call x1, Pallas kernels, per_device(): pl.pallas_call(functools.partial(kernel, nb, ns), out_shape=jax.ShapeDtyp...  47 us
    unnamed x1, local copies, waits for them, and re-layouts  1.87 us

profile of v2, /device:TPU:1, one launch (start us, length us, event | category | flops | bytes accessed | tf_op | source)
XLA Modules:
  0.0 48.9 jit_solution(7578950570602609940)
XLA Ops:
  0.0 47.0 %shard_map.37 = f32[32,32,128]{2,1,0:T(8,128)} custom-call(s32[32]{0:T(128)} %counts.1, f32[32,32,128]{2,1,0:T(8,128)} %source.1, f32[32,32,128]{2,1,0:T(8,128)} %beta.1), custom_call_target="tpu_custom_call" | custom-call | tf_op jit(solution)/shard_map/pallas_call | solution.py:663
  47.0 1.9 %copy.5 = f32[32,32,128]{2,1,0:T(8,128)} copy(f32[32,32,128]{2,1,0:T(8,128)} %shard_map.37) | data formatting | bytes 1048576

commit v3 on v2

--- a/solution.py
+++ b/solution.py
@@ -62,9 +62,9 @@
 def kernel(
     nb, ns,
     counts, source, beta, out,
-    b0, f0, u0, w0, r0, kx, ky, rs, xs0, xr0, e0m, e0x, e0y, c0, cx, cy, cz,
-    b1, f1, u1, v1, w1, xs1b, xr1b, xs1f, xr1f, y1, e1x,
-    b2, f2, u2, v2, w2, xs2b, xr2b, xs2f, xr2f, y2,
+    b0, f0, u0, w0, r0, kx, ky, rs, xs0, xr0, xc0, e0m, e0x, e0y, c0, cx, cy, cz,
+    b1, f1, u1, w1, xs1b, xr1b, xc1b, xs1f, xr1f, xc1f, y1, e1x,
+    b2, f2, u2, w2, y2,
     t3, tx, xa, ga, xb, gb_all, onehot, kx3, ky3, kz3, d3, i3, p3, r3, s3,
     in_sem, send_sem, recv_sem, zsend, zrecv, bsend, brecv,
 ):
@@ -81,25 +81,27 @@
     get_b.start()
     get_f.start()
 
+    core, chip, chips = lax.rem(me, 2), me // 2, nb // 2
+
+    def stack_peer(k):
+        return 2 * chip + lax.rem(core + k, 2), lax.rem(sub + k // 2, ns)
+
+    def chip_peer(k):
+        return 2 * lax.rem(chip + k, chips) + core, sub
+
     barrier = pltpu.get_barrier_semaphore()
 
-    def greet_sub(k, carry):
-        pl.semaphore_signal(
-            barrier, inc=1, device_id=(me, lax.rem(sub + k, ns)), device_id_type=MESH
-        )
-        return carry
-
-    def greet_box(k, carry):
-        pl.semaphore_signal(
-            barrier, inc=1, device_id=(lax.rem(me + k, nb), sub), device_id_type=MESH
-        )
-        return carry
-
-    lax.fori_loop(1, ns, greet_sub, 0)
-    lax.fori_loop(1, nb, greet_box, 0)
+    def greet(peer):
+        def body(k, carry):
+            pl.semaphore_signal(barrier, inc=1, device_id=peer(k), device_id_type=MESH)
+            return carry
+        return body
+
     for there in (left, right):
-        for level in (down, up):
+        for level in (down, sub, up):
             pl.semaphore_signal(barrier, inc=1, device_id=(there, level), device_id_type=MESH)
+    lax.fori_loop(1, 2 * ns, greet(stack_peer), 0)
+    lax.fori_loop(1, chips, greet(chip_peer), 0)
 
     width = 32 * counts[me]
     width_left = 32 * counts[left]
@@ -166,23 +168,24 @@
 
     def coarsen(x, scratch, step):
         planes, rows, _ = x.shape
-        pairs = x.reshape(planes // 2, 2, rows, 128)
-        scratch[...] = pairs[:, 0] + pairs[:, 1]
+        n = planes // 2
+        pairs = x.reshape(n, 2, rows, 128)
+        scratch[pl.ds(0, n)] = pairs[:, 0] + pairs[:, 1]
         y = (
-            scratch[:, pl.ds(0, rows // 2, stride=2), :]
-            + scratch[:, pl.ds(1, rows // 2, stride=2), :]
+            scratch[pl.ds(0, n), pl.ds(0, rows // 2, stride=2), :]
+            + scratch[pl.ds(0, n), pl.ds(1, rows // 2, stride=2), :]
         )
         odd = (iota(y.shape, 2) // step) % 2 == 1
         return y + jnp.where(odd, turn(y, step, 2), turn(y, 128 - step, 2))
 
-    def pack(x, tile_ref, group, reach):
-        planes, rows, _ = x.shape
-        at = iota((rows, 128), 1)
+    def pack(x, tile_ref, reach):
+        at = iota((16, 128), 1)
         keep = (at < reach) | ((at >= half - reach) & (at < half))
-        total = jnp.zeros((rows, 128), F32)
-        for z in range(planes):
-            total = total + turn(jnp.where(keep, x[z], 0.0), group * z, 1)
-        tile_ref[...] = total
+        for n in range(2):
+            total = jnp.zeros((16, 128), F32)
+            for z in range(8):
+                total = total + turn(jnp.where(keep, x[8 * n + z], 0.0), 16 * z, 1)
+            tile_ref[n] = total
 
     def to_slots(x):
         for z in range(4):
@@ -198,11 +201,9 @@
 
     each(4, 0, 16, pair_b)
     own_b1 = 0.125 * squeeze_level0()
-    b1[pl.ds(3, 16)] = own_b1
-    pack(own_b1, xs1b, 8, 3)
+    b1[pl.ds(6, 16)] = own_b1
+    pack(own_b1, xs1b, 6)
     own_b2 = 0.125 * coarsen(own_b1, y1, 1)
-    b2[pl.ds(3, 8)] = own_b2
-    pack(own_b2, xs2b, 16, 6)
 
     def couple(e):
         b = b0[e + 1]
@@ -234,17 +235,21 @@
 
     each(5, 2, 32, start_plane)
 
-    pl.semaphore_wait(barrier, (ns - 1) + (nb - 1) + 4)
-
-    def x_copies(src, dst, base):
+    pl.semaphore_wait(barrier, 6 + (2 * ns - 1) + (chips - 1))
+
+    def x_copies(src, dst, for_up, for_down, corner, base):
         made = []
         for side, there in ((0, right), (1, left)):
-            for slot, level in ((0, up), (1, sub), (2, down)):
-                n = base + side * 3 + slot
+            for n, (begin, end, level) in enumerate((
+                (src, dst.at[side], sub),
+                (for_up, corner.at[side, 0], up),
+                (for_down, corner.at[side, 1], down),
+            )):
+                at = base + side * 3 + n
                 made.append(
                     pltpu.make_async_remote_copy(
-                        src_ref=src, dst_ref=dst.at[side, slot],
-                        send_sem=send_sem.at[n], recv_sem=recv_sem.at[n],
+                        src_ref=begin, dst_ref=end,
+                        send_sem=send_sem.at[at], recv_sem=recv_sem.at[at],
                         device_id=(there, level), device_id_type=MESH,
                     )
                 )
@@ -272,22 +277,28 @@
         for copy in copies:
             copy.wait()
 
-    copies0 = x_copies(xs0, xr0, 0) + z_copies(b0, 32, 2, 6) + z_copies(f0, 32, 1, 8)
+    copies0 = x_copies(xs0, xr0, xs0.at[0], xs0.at[0], xc0, 0) + z_copies(b0, 32, 2, 6) + z_copies(f0, 32, 1, 8)
     start(copies0)
 
-    def sub_copy(k, which, slot):
+    def stack_copy(k, which, slot):
         return pltpu.make_async_remote_copy(
-            src_ref=xa.at[which], dst_ref=ga.at[which, slot],
+            src_ref=xa.at[which], dst_ref=ga.at[which, slot[0], slot[1]],
             send_sem=zsend.at[which, k], recv_sem=zrecv.at[which, k],
-            device_id=(me, lax.rem(sub + k, ns)), device_id_type=MESH,
-        )
-
-    def box_copy(k, which, slot):
+            device_id=stack_peer(k), device_id_type=MESH,
+        )
+
+    def chip_copy(k, which, slot):
         return pltpu.make_async_remote_copy(
-            src_ref=xb.at[which], dst_ref=gb_all.at[which, slot],
+            src_ref=xb.at[which], dst_ref=gb_all.at[which, pl.ds(2 * slot, 2)],
             send_sem=bsend.at[which, k], recv_sem=brecv.at[which, k],
-            device_id=(lax.rem(me + k, nb), sub), device_id_type=MESH,
-        )
+            device_id=chip_peer(k), device_id_type=MESH,
+        )
+
+    def stack_from(k):
+        return lax.rem(core + k, 2), lax.rem(sub - k // 2 + ns, ns)
+
+    def chip_from(k):
+        return lax.rem(chip - k + chips, chips)
 
     def send_all(make, which, mine, count):
         def body(k, carry):
@@ -295,9 +306,9 @@
             return carry
         lax.fori_loop(1, count, body, 0)
 
-    def wait_all(make, which, mine, count):
+    def wait_all(make, which, source, count):
         def body(k, carry):
-            copy = make(k, which, lax.rem(mine - k + count, count))
+            copy = make(k, which, source(k))
             copy.wait_send()
             copy.wait_recv()
             return carry
@@ -306,28 +317,28 @@
     def gather_start(x, which):
         tile = to_slots(x)
         xa[which] = tile
-        ga[which, sub] = tile
-        send_all(sub_copy, which, sub, ns)
+        ga[which, core, sub] = tile
+        send_all(stack_copy, which, (core, sub), 2 * ns)
 
     def gather_turn(which):
-        wait_all(sub_copy, which, sub, ns)
+        wait_all(stack_copy, which, stack_from, 2 * ns)
         at = (iota((16, lanes_n), 1) // 4) % ns
-        tile = jnp.zeros((16, lanes_n), F32)
-        for k in range(ns):
-            tile = jnp.where(at == k, ga[which, k], tile)
-        xb[which] = tile
-        gb_all[which, me] = tile
-        send_all(box_copy, which, me, nb)
+        for c in range(2):
+            tile = jnp.zeros((16, lanes_n), F32)
+            for k in range(ns):
+                tile = jnp.where(at == k, ga[which, c, k], tile)
+            xb[which, c] = tile
+            gb_all[which, 2 * chip + c] = tile
+        send_all(chip_copy, which, chip, chips)
 
     def gather_end(which):
-        wait_all(box_copy, which, me, nb)
+        wait_all(chip_copy, which, chip_from, chips)
         rows = gb_all[which].reshape(nb * 16, lanes_n)
         return pick_left(onehot[...], rows).reshape(vn, 8, lanes_n)
 
-    copies_b1 = x_copies(xs1b, xr1b, 10) + z_copies(b1, 16, 3, 16)
+    copies_b1 = x_copies(xs1b, xr1b, xs1b.at[1], xs1b.at[0], xc1b, 10)
+    copies_b1 = copies_b1 + z_copies(b1, 16, 6, 16)
     start(copies_b1)
-    copies_b2 = x_copies(xs2b, xr2b, 18) + z_copies(b2, 8, 3, 24)
-    start(copies_b2)
     gather_start(0.125 * coarsen(own_b2, y2, 2), 0)
 
     each(2, 1, 15, pair_r)
@@ -349,19 +360,18 @@
     turn_l1 = lax.rem(129 - width_left + 128, 128)
     turn_l2 = lax.rem(130 - width_left + 128, 128)
 
-    def ghost(slot, which, near_by):
-        from_left, from_right = xr0[0, slot, which], xr0[1, slot, which]
+    def ghost(from_left, from_right, near_by):
         shift_l = turn_l1 if near_by == 1 else turn_l2
         return jnp.where(
             q0, turn(from_left, shift_l, 1),
             jnp.where(q3, turn(from_right, lax.rem(width - near_by, 128), 1), 0.0),
         )
 
-    ghost_b = ghost(1, 0, 1)
-    ghost_b_low = jnp.where(floor, 0.0, ghost(0, 0, 1))
-    ghost_b_high = jnp.where(roof, 0.0, ghost(2, 0, 1))
-    ghost_b_far = ghost(1, 0, 2)
-    ghost_f = ghost(1, 1, 1)
+    ghost_b = ghost(xr0[0, 0], xr0[1, 0], 1)
+    ghost_b_low = jnp.where(floor, 0.0, ghost(xc0[0, 0], xc0[1, 0], 1))
+    ghost_b_high = jnp.where(roof, 0.0, ghost(xc0[0, 1], xc0[1, 1], 1))
+    ghost_b_far = ghost(xr0[0, 0], xr0[1, 0], 2)
+    ghost_f = ghost(xr0[0, 1], xr0[1, 1], 1)
     own_edge = jnp.where(q0 | q3, tb, 0.0)
     turned = width // 4 - 1
     first_z = (q0 & (group == 0)) | (q3 & (group == turned))
@@ -416,33 +426,39 @@
 
     each(4, 0, 16, mend)
 
-    def join(ref, xr, own, halo, gr, reach):
-        rows = ref.shape[1]
-        at = iota((rows, 128), 1)
+    def join(ref, xr, xc, halo):
+        at = iota((16, 128), 1)
         inside = at < half
-        keep = ((at >= half) & (at < half + reach)) | (at >= 128 - reach)
-        sub_at = at % gr
-        tiles = []
-        for slot in range(3):
-            from_left = turn(xr[0, slot], lax.rem(256 - half_left, 128), 1)
-            from_right = turn(xr[1, slot], half, 1)
-            tiles.append(
-                jnp.where(
-                    sub_at >= gr - reach, from_left, jnp.where(sub_at < reach, from_right, 0.0)
-                )
+        keep = ((at >= half) & (at < half + halo)) | (at >= 128 - halo)
+        sub_at = at % 16
+
+        def beside_own(from_left, from_right):
+            from_left = turn(from_left, lax.rem(256 - half_left, 128), 1)
+            from_right = turn(from_right, half, 1)
+            return jnp.where(
+                sub_at >= 16 - halo, from_left, jnp.where(sub_at < halo, from_right, 0.0)
             )
-        for z in range(-halo, own + halo):
-            slot = 0 if z < 0 else (2 if z >= own else 1)
-            there = z % own
+
+        tiles = [beside_own(xr[0, n], xr[1, n]) for n in range(2)]
+        low = beside_own(xc[0, 0], xc[1, 0])
+        high = beside_own(xc[0, 1], xc[1, 1])
+        for z in range(-halo, 16 + halo):
+            tile = low if z < 0 else (high if z >= 16 else tiles[z // 8])
             plane = jnp.where(
                 inside, ref[z + halo],
-                jnp.where(keep, turn(tiles[slot], (128 - gr * there) % 128, 1), 0.0),
+                jnp.where(keep, turn(tile, (128 - 16 * (z % 8)) % 128, 1), 0.0),
             )
             if z < 0:
                 plane = jnp.where(floor, 0.0, plane)
-            if z >= own:
+            if z >= 16:
                 plane = jnp.where(roof, 0.0, plane)
             ref[z + halo] = plane
+
+    def only_inside(x, out):
+        n = x.shape[0]
+        return jnp.concatenate([
+            jnp.where(floor, 0.0, x[:out]), x[out:n - out], jnp.where(roof, 0.0, x[n - out:])
+        ], 0)
 
     def weights(b, step):
         n = b.shape[0]
@@ -456,31 +472,30 @@
             around(v[1:n - 1], step) + v[:n - 2] + v[2:]
         )
 
-    def begin_level(b_ref, f_ref, w_ref, u_ref, v_ref, own, step):
-        w = w_ref[...]
-        u = w * f_ref[...]
+    def begin_level(b_ref, f_ref, w_ref, u_ref, step):
+        n = f_ref.shape[0]
+        f = f_ref[...]
+        u = w_ref[...] * f
         u_ref[...] = u
-        v = b_ref[pl.ds(1, own + 4)] * u
-        v_ref[...] = v
-        b = b_ref[pl.ds(3, own)]
-        gain = gain_of(b, u[1:own + 3], v[1:own + 3], step)
-        return REST * f_ref[pl.ds(2, own)] + 0.5 * gain
-
-    def end_level(b_ref, f_ref, w_ref, u, own, step):
-        v = b_ref[pl.ds(1, own + 4)] * u
-        b = b_ref[pl.ds(2, own + 2)]
+        v = b_ref[pl.ds(1, n)] * u
+        gain = gain_of(b_ref[pl.ds(2, n - 2)], u, v, step)
+        return REST * f[1:n - 1] + 0.5 * gain
+
+    def end_level(b_ref, f_ref, w_ref, u, step):
+        n = u.shape[0]
+        skip = (f_ref.shape[0] - n) // 2 + 1
+        v = b_ref[pl.ds(skip, n)] * u
+        b = b_ref[pl.ds(skip + 1, n - 2)]
         gain = gain_of(b, u, v, step)
-        e = REST * u[1:own + 3] + w_ref[pl.ds(1, own + 2)] * (
-            f_ref[pl.ds(1, own + 2)] + 0.5 * gain
-        )
-        return jnp.concatenate([
-            jnp.where(floor, 0.0, e[:1]), e[1:own + 1], jnp.where(roof, 0.0, e[own + 1:])
-        ], 0)
+        return only_inside(REST * u[1:n - 1] + w_ref[pl.ds(skip, n - 2)] * (
+            f_ref[pl.ds(skip, n - 2)] + 0.5 * gain
+        ), 1)
 
     own_f1 = 0.5 * squeeze_level0()
-    f1[pl.ds(2, 16)] = own_f1
-    pack(own_f1, xs1f, 8, 2)
-    copies_f1 = x_copies(xs1f, xr1f, 26) + z_copies(f1, 16, 2, 32)
+    f1[pl.ds(5, 16)] = own_f1
+    pack(own_f1, xs1f, 5)
+    copies_f1 = x_copies(xs1f, xr1f, xs1f.at[1], xs1f.at[0], xc1f, 18)
+    copies_f1 = copies_f1 + z_copies(f1, 16, 5, 24)
     start(copies_f1)
 
     def prepare(z, odd):
@@ -506,31 +521,21 @@
         prepare(2 * k + 1, True)
 
     gather_turn(0)
+    wait(copies_b1)
+    join(b1, xr1b, xc1b, 6)
+    w1[...] = weights(b1[...], 1)
+    b2[...] = 0.125 * coarsen(b1[...], y1, 1)
+    w2[...] = weights(b2[...], 2)
+
+    wait(copies_f1)
+    join(f1, xr1f, xc1f, 5)
+    r1 = begin_level(b1, f1, w1, u1, 1)
+    f2[...] = only_inside(0.5 * coarsen(r1, y1, 1), 2)
+    r2 = begin_level(b2, f2, w2, u2, 2)
+    gather_start(0.5 * coarsen(r2[1:9], y2, 2), 1)
     each(1, 0, 8, prepare_pair)
-    wait(copies_b1)
-    join(b1, xr1b, 16, 3, 8, 3)
-    w1[...] = weights(b1[...], 1)
-
-    wait(copies_f1)
-    join(f1, xr1f, 16, 2, 8, 2)
-    r1 = begin_level(b1, f1, w1, u1, v1, 16, 1)
-    own_f2 = 0.5 * coarsen(r1, y1, 1)
-    own_f2 = jnp.where(iota(own_f2.shape, 2) < half, own_f2, 0.0)
-    f2[pl.ds(2, 8)] = own_f2
-    pack(own_f2, xs2f, 16, 4)
-    copies_f2 = x_copies(xs2f, xr2f, 34) + z_copies(f2, 8, 2, 40)
-    start(copies_f2)
-
+    gather_turn(1)
     each(1, 8, 16, prepare_pair)
-    wait(copies_b2)
-    join(b2, xr2b, 8, 3, 16, 6)
-    w2[...] = weights(b2[...], 2)
-
-    wait(copies_f2)
-    join(f2, xr2f, 8, 2, 16, 4)
-    r2 = begin_level(b2, f2, w2, u2, v2, 8, 2)
-    gather_start(0.5 * coarsen(r2, y2, 2), 1)
-    gather_turn(1)
 
     not_top = iota((vn, 8, lanes_n), 2) % nz3 < nz3 - 1
 
@@ -601,11 +606,11 @@
     e3 = pick_left_t(from_row, by_lane).reshape(6, 1, 8, 128)
     e3 = jnp.broadcast_to(e3, (6, 2, 8, 128)).reshape(12, 8, 128)
 
-    e2 = end_level(b2, f2, w2, u2[...] + e3, 8, 2)
+    e2 = end_level(b2, f2, w2, u2[...] + e3, 2)
     e1x[:, pl.ds(0, 8, stride=2), :] = e2
     e1x[:, pl.ds(1, 8, stride=2), :] = e2
     grown = jnp.broadcast_to(e1x[...].reshape(10, 1, 16, 128), (10, 2, 16, 128))
-    e1 = end_level(b1, f1, w1, u1[...] + grown.reshape(20, 16, 128), 16, 1)
+    e1 = end_level(b1, f1, w1, u1[pl.ds(3, 20)] + grown.reshape(20, 16, 128), 1)
 
     si, sc = iota((128, 256), 0), iota((128, 256), 1)
     sx = sc - 128
@@ -644,21 +649,21 @@
     scratch = [
         vmem(36, 32, 128), vmem(34, 32, 128), vmem(34, 32, 128), vmem(34, 32, 128),
         vmem(32, 32, 128), vmem(34, 32, 128), vmem(34, 32, 128),
-        vmem(16, 32, 128), vmem(2, 32, 128), vmem(2, 3, 2, 32, 128),
+        vmem(16, 32, 128), vmem(2, 32, 128), vmem(2, 2, 32, 128), vmem(2, 2, 32, 128),
         vmem(18, 32, 128), vmem(18, 32, 128), vmem(18, 32, 128),
         vmem(32, 32, 128), vmem(32, 32, 128), vmem(32, 32, 128), vmem(32, 32, 128),
-        vmem(22, 16, 128), vmem(20, 16, 128), vmem(20, 16, 128), vmem(20, 16, 128),
-        vmem(20, 16, 128), vmem(16, 128), vmem(2, 3, 16, 128), vmem(16, 128), vmem(2, 3, 16, 128), vmem(8, 16, 128),
-        vmem(10, 16, 128),
-        vmem(14, 8, 128), vmem(12, 8, 128), vmem(12, 8, 128), vmem(12, 8, 128),
-        vmem(12, 8, 128), vmem(8, 128), vmem(2, 3, 8, 128), vmem(8, 128), vmem(2, 3, 8, 128), vmem(4, 8, 128),
-        vmem(32, 128), vmem(128, lanes_n), vmem(2, 16, lanes_n), vmem(2, ns, 16, lanes_n),
-        vmem(2, 16, lanes_n), vmem(2, nb, 16, lanes_n), vmem(8 * nb, 16 * nb, dtype=BF16),
+        vmem(28, 16, 128), vmem(26, 16, 128), vmem(26, 16, 128), vmem(26, 16, 128),
+        vmem(2, 16, 128), vmem(2, 2, 16, 128), vmem(2, 2, 16, 128),
+        vmem(2, 16, 128), vmem(2, 2, 16, 128), vmem(2, 2, 16, 128),
+        vmem(14, 16, 128), vmem(10, 16, 128),
+        vmem(14, 8, 128), vmem(12, 8, 128), vmem(12, 8, 128), vmem(12, 8, 128), vmem(4, 8, 128),
+        vmem(32, 128), vmem(128, lanes_n), vmem(2, 16, lanes_n), vmem(2, 2, ns, 16, lanes_n),
+        vmem(2, 2, 16, lanes_n), vmem(2, nb, 16, lanes_n), vmem(8 * nb, 16 * nb, dtype=BF16),
         coarse(), coarse(), coarse(), coarse(), coarse(), coarse(), coarse(), coarse(),
         pltpu.SemaphoreType.DMA((2,)),
-        pltpu.SemaphoreType.DMA((42,)), pltpu.SemaphoreType.DMA((42,)),
-        pltpu.SemaphoreType.DMA((2, ns)), pltpu.SemaphoreType.DMA((2, ns)),
-        pltpu.SemaphoreType.DMA((2, nb)), pltpu.SemaphoreType.DMA((2, nb)),
+        pltpu.SemaphoreType.DMA((26,)), pltpu.SemaphoreType.DMA((26,)),
+        pltpu.SemaphoreType.DMA((2, 2 * ns)), pltpu.SemaphoreType.DMA((2, 2 * ns)),
+        pltpu.SemaphoreType.DMA((2, nb // 2)), pltpu.SemaphoreType.DMA((2, nb // 2)),
     ]
     return pl.pallas_call(
         functools.partial(kernel, nb, ns),

time: 49.1 us -> 43.7 us (0.89)
  Pallas kernels: 47 us -> 41.6 us
    pallas_call x1, Pallas kernels: 47 us -> 41.6 us  [per_device(): pl.pallas_call(functools.partial(kernel, nb, ns), out_shape=jax.ShapeDtyp...]
where the time goes in v3:
time: 43.7 us; the launch traced here: 43.5 us
  Pallas kernels  41.6 us (95%)
  local copies, waits for them, and re-layouts  1.87 us (4%)
    pallas_call x1, Pallas kernels, per_device(): pl.pallas_call(functools.partial(kernel, nb, ns), out_shape=jax.ShapeDtyp...  41.6 us
    unnamed x1, local copies, waits for them, and re-layouts  1.87 us

profile of v3, /device:TPU:1, one launch (start us, length us, event | category | flops | bytes accessed | tf_op | source)
XLA Modules:
  0.0 43.5 jit_solution(11656181473944673110)
XLA Ops:
  0.0 41.6 %shard_map.37 = f32[32,32,128]{2,1,0:T(8,128)} custom-call(s32[32]{0:T(128)} %counts.1, f32[32,32,128]{2,1,0:T(8,128)} %source.1, f32[32,32,128]{2,1,0:T(8,128)} %beta.1), custom_call_target="tpu_custom_call" | custom-call | tf_op jit(solution)/shard_map/pallas_call | solution.py:668
  41.7 1.9 %copy.5 = f32[32,32,128]{2,1,0:T(8,128)} copy(f32[32,32,128]{2,1,0:T(8,128)} %shard_map.37) | data formatting | bytes 1048576

commit v4 on v3

--- a/solution.py
+++ b/solution.py
@@ -62,10 +62,10 @@
 def kernel(
     nb, ns,
     counts, source, beta, out,
-    b0, f0, u0, w0, r0, kx, ky, rs, xs0, xr0, xc0, e0m, e0x, e0y, c0, cx, cy, cz,
+    b0, f0, u0, w0, r0, kx, ky, rs, xs0, xr0, xd0, xc0, e0m, e0x, e0y, c0, cx, cy, cz,
     b1, f1, u1, w1, xs1b, xr1b, xc1b, xs1f, xr1f, xc1f, y1, e1x,
     b2, f2, u2, w2, y2,
-    t3, tx, xa, ga, xb, gb_all, onehot, kx3, ky3, kz3, d3, i3, p3, r3, s3,
+    t3, tx, xa, ga, xb, gb_all, onehot, kx3, ky3, kz3, d3, i3, p3, m3, r3, s3,
     in_sem, send_sem, recv_sem, zsend, zrecv, bsend, brecv,
 ):
     lanes_n = 16 * ns
@@ -108,7 +108,7 @@
     half = width // 2
     half_left = width_left // 2
     kk = iota((1, nb * 16), 1)
-    kd, kj = kk // 16, kk % 16
+    kd, kj = kk // 16, (kk % 16) // ns * ns + ns - 1 - kk % ns
 
     def place(d, carry):
         where_from, begin, mine = carry
@@ -160,6 +160,13 @@
     tb, tf = lax.fori_loop(0, 8, load_planes, (zero_tile, zero_tile))
     xs0[0] = tb
     xs0[1] = tf
+    for n, z in ((0, 0), (1, 31)):
+        corner = jnp.zeros((8, 128), F32)
+        for m, shift in ((0, (128 - 4 * z) % 128), (4, lax.rem(389 - 4 * z - width, 128))):
+            column = jnp.where(lane == m, turn(tb, shift, 1), 0.0)
+            for q in range(4):
+                corner = corner + turn(column[8 * q:8 * q + 8], q, 1)
+        xd0[n] = corner
 
 
     def squeeze_level0():
@@ -277,7 +284,7 @@
         for copy in copies:
             copy.wait()
 
-    copies0 = x_copies(xs0, xr0, xs0.at[0], xs0.at[0], xc0, 0) + z_copies(b0, 32, 2, 6) + z_copies(f0, 32, 1, 8)
+    copies0 = x_copies(xs0, xr0, xd0.at[1], xd0.at[0], xc0, 0) + z_copies(b0, 32, 2, 6) + z_copies(f0, 32, 1, 8)
     start(copies0)
 
     def stack_copy(k, which, slot):
@@ -314,21 +321,30 @@
             return carry
         lax.fori_loop(1, count, body, 0)
 
+    slot_at = (iota((ns, lanes_n), 1) // 4) % ns
+    row_at = iota((ns, lanes_n), 0)
+
     def gather_start(x, which):
         tile = to_slots(x)
-        xa[which] = tile
-        ga[which, core, sub] = tile
+        for h in range(16 // ns):
+            part = jnp.where(row_at == slot_at, tile[h * ns:(h + 1) * ns], 0.0)
+            part = jnp.sum(part, axis=0, keepdims=True)
+            xa[which, pl.ds(h, 1)] = part
+            ga[which, core, sub, pl.ds(h, 1)] = part
         send_all(stack_copy, which, (core, sub), 2 * ns)
 
     def gather_turn(which):
         wait_all(stack_copy, which, stack_from, 2 * ns)
-        at = (iota((16, lanes_n), 1) // 4) % ns
         for c in range(2):
-            tile = jnp.zeros((16, lanes_n), F32)
-            for k in range(ns):
-                tile = jnp.where(at == k, ga[which, c, k], tile)
-            xb[which, c] = tile
-            gb_all[which, 2 * chip + c] = tile
+            for h in range(16 // ns):
+                tile = jnp.zeros((ns, lanes_n), F32)
+                for k in range(ns):
+                    part = jnp.broadcast_to(ga[which, c, k, pl.ds(h, 1)], (ns, lanes_n))
+                    part = pltpu.roll(part, 0, 1, stride=4, stride_axis=0)
+                    part = turn(part, (4 * (k - ns + 1)) % lanes_n, 1)
+                    tile = jnp.where(slot_at == k, part, tile)
+                xb[which, c, pl.ds(h * ns, ns)] = tile
+                gb_all[which, 2 * chip + c, pl.ds(h * ns, ns)] = tile
         send_all(chip_copy, which, chip, chips)
 
     def gather_end(which):
@@ -368,8 +384,21 @@
         )
 
     ghost_b = ghost(xr0[0, 0], xr0[1, 0], 1)
-    ghost_b_low = jnp.where(floor, 0.0, ghost(xc0[0, 0], xc0[1, 0], 1))
-    ghost_b_high = jnp.where(roof, 0.0, ghost(xc0[0, 1], xc0[1, 1], 1))
+
+    def ghost_corner(n, z, outside):
+        from_left, from_right = xc0[0, n], xc0[1, n]
+        rows = []
+        for q in range(4):
+            at_left = turn(from_left, (128 + 4 * z - 4 - q) % 128, 1)
+            at_right = turn(from_right, lax.rem(4 * z + width + 127 - q, 128), 1)
+            rows.append(jnp.where(
+                lane[:8] == 4 * z, at_left,
+                jnp.where(lane[:8] == lax.rem(4 * z + width - 1, 128), at_right, 0.0),
+            ))
+        return jnp.where(outside, 0.0, jnp.concatenate(rows, 0))
+
+    ghost_b_low = ghost_corner(0, 31, floor)
+    ghost_b_high = ghost_corner(1, 0, roof)
     ghost_b_far = ghost(xr0[0, 0], xr0[1, 0], 2)
     ghost_f = ghost(xr0[0, 1], xr0[1, 1], 1)
     own_edge = jnp.where(q0 | q3, tb, 0.0)
@@ -565,9 +594,9 @@
 
     coarse_f = gather_end(1)
     r3[...] = coarse_f
-    first_p = coarse_f * i3[...]
-    p3[...] = first_p
     s3[...] = jnp.zeros((vn, 8, lanes_n), F32)
+    p3[...] = jnp.zeros((vn, 8, lanes_n), F32)
+    m3[...] = jnp.zeros((vn, 8, lanes_n), F32)
 
     def image(p):
         px, py, pz = kx3[...], ky3[...], kz3[...]
@@ -577,21 +606,25 @@
             + pz * turn(p, lanes_n - 1, 2) + turn(pz * p, 1, 2)
         )
 
-    def iterate(n, rz):
-        p = p3[...]
-        q = image(p)
-        alpha = rz / total3(p * q)
+    def iterate(n, carry):
+        gamma_old, alpha_old = carry
+        r = r3[...]
+        z = r * i3[...]
+        az = image(z)
+        gamma, delta = total3(r * z), total3(z * az)
+        beta = jnp.where(n == 0, 0.0, gamma / gamma_old)
+        alpha = gamma / (delta - beta * gamma / alpha_old)
+        p = z + beta * p3[...]
+        q = az + beta * m3[...]
+        p3[...] = p
+        m3[...] = q
         s3[...] = s3[...] + alpha * p
-        r = r3[...] - alpha * q
-        r3[...] = r
-        scaled = r * i3[...]
-        new = total3(r * scaled)
-        p3[...] = scaled + (new / rz) * p
-        return new
-
-    rz = lax.fori_loop(0, SWEEPS - 1, iterate, total3(coarse_f * first_p))
-    last_p = p3[...]
-    solved = s3[...] + (rz / total3(last_p * image(last_p))) * last_p
+        r3[...] = r - alpha * q
+        return gamma, alpha
+
+    one = jnp.ones((1, 1), F32)
+    lax.fori_loop(0, SWEEPS, iterate, (one, one))
+    solved = s3[...]
 
     l_at, k_at = iota((128, 8 * vn), 0), iota((128, 8 * vn), 1)
     relative = jnp.where(l_at < 124, l_at // 4, -1)
@@ -649,7 +682,7 @@
     scratch = [
         vmem(36, 32, 128), vmem(34, 32, 128), vmem(34, 32, 128), vmem(34, 32, 128),
         vmem(32, 32, 128), vmem(34, 32, 128), vmem(34, 32, 128),
-        vmem(16, 32, 128), vmem(2, 32, 128), vmem(2, 2, 32, 128), vmem(2, 2, 32, 128),
+        vmem(16, 32, 128), vmem(2, 32, 128), vmem(2, 2, 32, 128), vmem(2, 8, 128), vmem(2, 2, 8, 128),
         vmem(18, 32, 128), vmem(18, 32, 128), vmem(18, 32, 128),
         vmem(32, 32, 128), vmem(32, 32, 128), vmem(32, 32, 128), vmem(32, 32, 128),
         vmem(28, 16, 128), vmem(26, 16, 128), vmem(26, 16, 128), vmem(26, 16, 128),
@@ -657,9 +690,9 @@
         vmem(2, 16, 128), vmem(2, 2, 16, 128), vmem(2, 2, 16, 128),
         vmem(14, 16, 128), vmem(10, 16, 128),
         vmem(14, 8, 128), vmem(12, 8, 128), vmem(12, 8, 128), vmem(12, 8, 128), vmem(4, 8, 128),
-        vmem(32, 128), vmem(128, lanes_n), vmem(2, 16, lanes_n), vmem(2, 2, ns, 16, lanes_n),
+        vmem(32, 128), vmem(128, lanes_n), vmem(2, 16 // ns, lanes_n), vmem(2, 2, ns, 16 // ns, lanes_n),
         vmem(2, 2, 16, lanes_n), vmem(2, nb, 16, lanes_n), vmem(8 * nb, 16 * nb, dtype=BF16),
-        coarse(), coarse(), coarse(), coarse(), coarse(), coarse(), coarse(), coarse(),
+        coarse(), coarse(), coarse(), coarse(), coarse(), coarse(), coarse(), coarse(), coarse(),
         pltpu.SemaphoreType.DMA((2,)),
         pltpu.SemaphoreType.DMA((26,)), pltpu.SemaphoreType.DMA((26,)),
         pltpu.SemaphoreType.DMA((2, 2 * ns)), pltpu.SemaphoreType.DMA((2, 2 * ns)),

time: 43.7 us -> 41.2 us (0.943)
  Pallas kernels: 41.6 us -> 38.8 us
    pallas_call x1, Pallas kernels: 41.6 us -> 38.8 us  [per_device(): pl.pallas_call(functools.partial(kernel, nb, ns), out_shape=jax.ShapeDtyp...]
where the time goes in v4:
time: 41.2 us; the launch traced here: 40.7 us
  Pallas kernels  38.8 us (94%)
  local copies, waits for them, and re-layouts  1.87 us (5%)
    pallas_call x1, Pallas kernels, per_device(): pl.pallas_call(functools.partial(kernel, nb, ns), out_shape=jax.ShapeDtyp...  38.8 us
    unnamed x1, local copies, waits for them, and re-layouts  1.87 us

profile of v4, /device:TPU:1, one launch (start us, length us, event | category | flops | bytes accessed | tf_op | source)
XLA Modules:
  0.0 40.7 jit_solution(15087842964137933196)
XLA Ops:
  0.0 38.8 %shard_map.37 = f32[32,32,128]{2,1,0:T(8,128)} custom-call(s32[32]{0:T(128)} %counts.1, f32[32,32,128]{2,1,0:T(8,128)} %source.1, f32[32,32,128]{2,1,0:T(8,128)} %beta.1), custom_call_target="tpu_custom_call" | custom-call | tf_op jit(solution)/shard_map/pallas_call | solution.py:701
  38.8 1.9 %copy.5 = f32[32,32,128]{2,1,0:T(8,128)} copy(f32[32,32,128]{2,1,0:T(8,128)} %shard_map.37) | data formatting | bytes 1048576

commit v5 on v4

--- a/solution.py
+++ b/solution.py
@@ -18,10 +18,8 @@
 
 def split(x):
     high = x.astype(BF16)
-    rest = x - high.astype(F32)
-    middle = rest.astype(BF16)
-    low = (rest - middle.astype(F32)).astype(BF16)
-    return (high, middle, low)
+    middle = (x - high.astype(F32)).astype(BF16)
+    return (high, middle)
 
 
 def pick_right(x, chosen):
@@ -240,7 +238,6 @@
     def pair_r(k):
         rs[k] = residual(2 * k) + residual(2 * k + 1)
 
-    each(5, 2, 32, start_plane)
 
     pl.semaphore_wait(barrier, 6 + (2 * ns - 1) + (chips - 1))
 
@@ -355,8 +352,8 @@
     copies_b1 = x_copies(xs1b, xr1b, xs1b.at[1], xs1b.at[0], xc1b, 10)
     copies_b1 = copies_b1 + z_copies(b1, 16, 6, 16)
     start(copies_b1)
-    gather_start(0.125 * coarsen(own_b2, y2, 2), 0)
-
+
+    each(5, 2, 32, start_plane)
     each(2, 1, 15, pair_r)
     wait(copies0)
 
@@ -526,6 +523,7 @@
     copies_f1 = x_copies(xs1f, xr1f, xs1f.at[1], xs1f.at[0], xc1f, 18)
     copies_f1 = copies_f1 + z_copies(f1, 16, 5, 24)
     start(copies_f1)
+    gather_start(0.125 * coarsen(own_b2, y2, 2), 0)
 
     def prepare(z, odd):
         e = z + 1
@@ -549,7 +547,6 @@
         prepare(2 * k, False)
         prepare(2 * k + 1, True)
 
-    gather_turn(0)
     wait(copies_b1)
     join(b1, xr1b, xc1b, 6)
     w1[...] = weights(b1[...], 1)
@@ -562,6 +559,7 @@
     f2[...] = only_inside(0.5 * coarsen(r1, y1, 1), 2)
     r2 = begin_level(b2, f2, w2, u2, 2)
     gather_start(0.5 * coarsen(r2[1:9], y2, 2), 1)
+    gather_turn(0)
     each(1, 0, 8, prepare_pair)
     gather_turn(1)
     each(1, 8, 16, prepare_pair)
@@ -612,7 +610,7 @@
         z = r * i3[...]
         az = image(z)
         gamma, delta = total3(r * z), total3(z * az)
-        beta = jnp.where(n == 0, 0.0, gamma / gamma_old)
+        beta = 0.0 if n == 0 else gamma / gamma_old
         alpha = gamma / (delta - beta * gamma / alpha_old)
         p = z + beta * p3[...]
         q = az + beta * m3[...]
@@ -623,7 +621,9 @@
         return gamma, alpha
 
     one = jnp.ones((1, 1), F32)
-    lax.fori_loop(0, SWEEPS, iterate, (one, one))
+    carry = (one, one)
+    for n in range(SWEEPS):
+        carry = iterate(n, carry)
     solved = s3[...]
 
     l_at, k_at = iota((128, 8 * vn), 0), iota((128, 8 * vn), 1)

time: 41.2 us -> 40.1 us (0.973)
  Pallas kernels: 38.8 us -> 38 us
    pallas_call x1, Pallas kernels: 38.8 us -> 38 us  [per_device(): pl.pallas_call(functools.partial(kernel, nb, ns), out_shape=jax.ShapeDtyp...]
where the time goes in v5:
time: 40.1 us; the launch traced here: 39.9 us
  Pallas kernels  38 us (95%)
  local copies, waits for them, and re-layouts  1.87 us (5%)
    pallas_call x1, Pallas kernels, per_device(): pl.pallas_call(functools.partial(kernel, nb, ns), out_shape=jax.ShapeDtyp...  38 us
    unnamed x1, local copies, waits for them, and re-layouts  1.87 us

profile of v5, /device:TPU:1, one launch (start us, length us, event | category | flops | bytes accessed | tf_op | source)
XLA Modules:
  0.0 39.9 jit_solution(10336566344051297378)
XLA Ops:
  0.0 38.0 %shard_map.37 = f32[32,32,128]{2,1,0:T(8,128)} custom-call(s32[32]{0:T(128)} %counts.1, f32[32,32,128]{2,1,0:T(8,128)} %source.1, f32[32,32,128]{2,1,0:T(8,128)} %beta.1), custom_call_target="tpu_custom_call" | custom-call | tf_op jit(solution)/shard_map/pallas_call | solution.py:701
  38.0 1.9 %copy.5 = f32[32,32,128]{2,1,0:T(8,128)} copy(f32[32,32,128]{2,1,0:T(8,128)} %shard_map.37) | data formatting | bytes 1048576

commit v6 on v5

--- a/solution.py
+++ b/solution.py
@@ -196,7 +196,7 @@
         for z in range(4):
             t3[pl.ds(z, 4, stride=8), :] = x[z]
             t3[pl.ds(z + 4, 4, stride=8), :] = x[z]
-        tiles = t3[...].reshape(4, 1, 8, 128)
+        tiles = t3[pl.ds(0, 32)].reshape(4, 1, 8, 128)
         tiles = jnp.broadcast_to(tiles, (4, ns // 2, 8, 128)).reshape(lanes_n, 128)
         tx[...] = jnp.transpose(tiles)
         return tx[pl.ds(0, 16, stride=4), :]
@@ -689,8 +689,8 @@
         vmem(2, 16, 128), vmem(2, 2, 16, 128), vmem(2, 2, 16, 128),
         vmem(2, 16, 128), vmem(2, 2, 16, 128), vmem(2, 2, 16, 128),
         vmem(14, 16, 128), vmem(10, 16, 128),
-        vmem(14, 8, 128), vmem(12, 8, 128), vmem(12, 8, 128), vmem(12, 8, 128), vmem(4, 8, 128),
-        vmem(32, 128), vmem(128, lanes_n), vmem(2, 16 // ns, lanes_n), vmem(2, 2, ns, 16 // ns, lanes_n),
+        vmem(14, 8, 128), vmem(12, 8, 128), vmem(12, 8, 128), vmem(12, 8, 128), vmem(6, 8, 128),
+        vmem(72, 128), vmem(128, lanes_n), vmem(6, 16 // ns, lanes_n), vmem(3, 2, ns, 16 // ns, lanes_n),
         vmem(2, 2, 16, lanes_n), vmem(2, nb, 16, lanes_n), vmem(8 * nb, 16 * nb, dtype=BF16),
         coarse(), coarse(), coarse(), coarse(), coarse(), coarse(), coarse(), coarse(), coarse(),
         pltpu.SemaphoreType.DMA((2,)),

time: 40.1 us -> 40.1 us (level)
  no operation moved by 1% of the time
where the time goes in v6:
time: 40.1 us; the launch traced here: 39.9 us
  Pallas kernels  38 us (95%)
  local copies, waits for them, and re-layouts  1.87 us (5%)
    pallas_call x1, Pallas kernels, per_device(): pl.pallas_call(functools.partial(kernel, nb, ns), out_shape=jax.ShapeDtyp...  38 us
    unnamed x1, local copies, waits for them, and re-layouts  1.87 us

profile of v6, /device:TPU:1, one launch (start us, length us, event | category | flops | bytes accessed | tf_op | source)
XLA Modules:
  0.0 39.9 jit_solution(15184816313450126972)
XLA Ops:
  0.0 38.0 %shard_map.37 = f32[32,32,128]{2,1,0:T(8,128)} custom-call(s32[32]{0:T(128)} %counts.1, f32[32,32,128]{2,1,0:T(8,128)} %source.1, f32[32,32,128]{2,1,0:T(8,128)} %beta.1), custom_call_target="tpu_custom_call" | custom-call | tf_op jit(solution)/shard_map/pallas_call | solution.py:701
  38.0 1.9 %copy.5 = f32[32,32,128]{2,1,0:T(8,128)} copy(f32[32,32,128]{2,1,0:T(8,128)} %shard_map.37) | data formatting | bytes 1048576

commit v7 on v6

--- a/solution.py
+++ b/solution.py
@@ -98,8 +98,10 @@
     for there in (left, right):
         for level in (down, sub, up):
             pl.semaphore_signal(barrier, inc=1, device_id=(there, level), device_id_type=MESH)
-    lax.fori_loop(1, 2 * ns, greet(stack_peer), 0)
-    lax.fori_loop(1, chips, greet(chip_peer), 0)
+    for k in range(2 * ns - 1, 0, -1):
+        greet(stack_peer)(k, 0)
+    for k in range(1, chips):
+        greet(chip_peer)(k, 0)
 
     width = 32 * counts[me]
     width_left = 32 * counts[left]
@@ -450,7 +452,7 @@
     def mend(k):
         rs[k] = rs[k] + jnp.where(edge_two, back(gap_pair, 2 * k), 0.0)
 
-    each(4, 0, 16, mend)
+    each(16, 0, 16, mend)
 
     def join(ref, xr, xc, halo):
         at = iota((16, 128), 1)
@@ -605,20 +607,20 @@
         )
 
     def iterate(n, carry):
-        gamma_old, alpha_old = carry
+        over_gamma, over_alpha = carry
         r = r3[...]
         z = r * i3[...]
         az = image(z)
         gamma, delta = total3(r * z), total3(z * az)
-        beta = 0.0 if n == 0 else gamma / gamma_old
-        alpha = gamma / (delta - beta * gamma / alpha_old)
+        beta = 0.0 if n == 0 else gamma * over_gamma
+        alpha = gamma / (delta - beta * gamma * over_alpha)
         p = z + beta * p3[...]
         q = az + beta * m3[...]
         p3[...] = p
         m3[...] = q
         s3[...] = s3[...] + alpha * p
         r3[...] = r - alpha * q
-        return gamma, alpha
+        return 1.0 / gamma, 1.0 / alpha
 
     one = jnp.ones((1, 1), F32)
     carry = (one, one)

time: 40.1 us -> 39.6 us (0.988)
    pallas_call x1, Pallas kernels: 38 us -> 37.6 us  [per_device(): pl.pallas_call(functools.partial(kernel, nb, ns), out_shape=jax.ShapeDtyp...]
where the time goes in v7:
time: 39.6 us; the launch traced here: 39.5 us
  Pallas kernels  37.6 us (95%)
  local copies, waits for them, and re-layouts  1.87 us (5%)
    pallas_call x1, Pallas kernels, per_device(): pl.pallas_call(functools.partial(kernel, nb, ns), out_shape=jax.ShapeDtyp...  37.6 us
    unnamed x1, local copies, waits for them, and re-layouts  1.87 us

profile of v7, /device:TPU:1, one launch (start us, length us, event | category | flops | bytes accessed | tf_op | source)
XLA Modules:
  0.0 39.5 jit_solution(7284505595358933751)
XLA Ops:
  0.0 37.6 %shard_map.37 = f32[32,32,128]{2,1,0:T(8,128)} custom-call(s32[32]{0:T(128)} %counts.1, f32[32,32,128]{2,1,0:T(8,128)} %source.1, f32[32,32,128]{2,1,0:T(8,128)} %beta.1), custom_call_target="tpu_custom_call" | custom-call | tf_op jit(solution)/shard_map/pallas_call | solution.py:703
  37.6 1.9 %copy.5 = f32[32,32,128]{2,1,0:T(8,128)} copy(f32[32,32,128]{2,1,0:T(8,128)} %shard_map.37) | data formatting | bytes 1048576
